TPU v7x, 32 devices: a whole 2x2x4 slice. The times are simulated.
32 devices in a mesh: dp: 2 (over x), row: 4 (over y, core), col: 4 (over z).
Axes of the slice: x: 2, y: 2, z: 4, core: 2. Of those that a mesh axis runs over, the one named last changes fastest.
Arguments:
- inputs: bfloat16 [2, 512, 4096], P('dp', 'col', 'row'), may hold values from -6 to 6
- weights: bfloat16 [4096, 3, 4096], P('row', None, 'col'), may hold values from -0.09375 to 0.09375
- feature_taps: float32 [3, 3, 4096], P(None, None, 'col'), may hold values from -2.5 to 2.5
- inner_taps: float32 [7, 4096], P(None, 'col'), may hold values from -2.5 to 2.5
- grad_out: bfloat16 [2, 512, 4096], P('dp', 'row', 'col'), may hold values from -6 to 6
Outputs:
- grad_in: bfloat16 [2, 512, 4096], P('dp', 'col', 'row')
- grad_weights: float32 [4096, 3, 4096], P('row', None, 'col')
All inputs are finite; a program needn't handle non-finite values.
Results may differ from a plain program's by a relative error of at most 0.033.
Values may be sent and summed in bfloat16 or wider, within the bound.
No kernel may reach another device: no remote copies, remote signals or barrier semaphores. Data moves between devices by JAX's collectives and lax.ppermute only.
A program may use at most 128 MiB of HBM per device.

v0:
```python
import math

import jax
import jax.numpy as jnp
from jax import lax
from jax.experimental import pallas as pl
from jax.experimental.pallas import tpu as pltpu
from jax.sharding import PartitionSpec as P

LANES = 128
PAD = 8
CORES = 2


def shifted(shard, axis, by):
    length = lax.axis_size(axis)
    pairs = [(i, i + by) for i in range(length) if 0 <= i + by < length]
    return lax.ppermute(shard, axis, pairs)


def with_halo(cells, axis, width):
    head = shifted(cells[:width], axis, -1)
    tail = shifted(cells[-width:], axis, 1)
    return jnp.concatenate([tail, cells, head], axis=0)


def causal(seq, taps):
    total = taps[0] * seq
    for lag in range(1, taps.shape[0]):
        pad = jnp.zeros((lag,) + seq.shape[1:], jnp.float32)
        total = total + taps[lag] * jnp.concatenate([pad, seq[:-lag]], axis=0)
    return total


def anticausal(seq, taps):
    total = taps[0] * seq
    for lag in range(1, taps.shape[0]):
        pad = jnp.zeros((lag,) + seq.shape[1:], jnp.float32)
        total = total + taps[lag] * jnp.concatenate([seq[lag:], pad], axis=0)
    return total


def rounded(value):
    return lax.optimization_barrier(value.astype(jnp.bfloat16)).astype(jnp.float32)


def by_tokens(inputs, weights, feature_taps, inner_taps, grad_out):
    tile = inputs[0]
    upstream_tile = grad_out[0]
    rows_dev = upstream_tile.shape[0]
    width_row = weights.shape[0]
    width_col = weights.shape[2]
    margin = feature_taps.shape[0] - 1 + (inner_taps.shape[0] - 1)
    flat_w = weights.reshape(width_row, 3 * width_col)
    columns = lax.all_gather(tile, "col", axis=0, tiled=True)
    proj = lax.psum_scatter(
        jnp.dot(columns, flat_w, preferred_element_type=jnp.float32).astype(jnp.bfloat16),
        "row",
        scatter_dimension=0,
        tiled=True,
    )
    length = rows_dev + 2 * margin
    window = with_halo(proj, "row", margin).astype(jnp.float32).reshape(length, 3, width_col)
    after = shifted(upstream_tile[:margin], "row", -1)
    upstream = jnp.concatenate(
        [
            jnp.zeros((margin, width_col), jnp.float32),
            upstream_tile.astype(jnp.float32),
            after.astype(jnp.float32),
        ],
        axis=0,
    )
    mixed = causal(window, feature_taps)
    query = mixed[:, 0]
    key = mixed[:, 1]
    value = mixed[:, 2]
    product = rounded(key * value)
    inner = causal(product, inner_taps)
    grad_query = upstream * inner
    grad_product = anticausal(upstream * query, inner_taps)
    grad_mixed = jnp.stack([grad_query, grad_product * value, grad_product * key], axis=1)
    grad_proj = anticausal(grad_mixed, feature_taps)[margin : margin + rows_dev].astype(
        jnp.bfloat16
    )
    gathered = lax.all_gather(grad_proj.reshape(rows_dev, 3 * width_col), "row", axis=0, tiled=True)
    grad_x = lax.psum_scatter(
        lax.dot_general(
            gathered, flat_w, (((1,), (1,)), ((), ())), preferred_element_type=jnp.float32
        ).astype(jnp.bfloat16),
        "col",
        scatter_dimension=0,
        tiled=True,
    )
    local = lax.dot_general(
        columns, gathered, (((0,), (0,)), ((), ())), preferred_element_type=jnp.float32
    )
    grad_w = lax.psum(local.astype(jnp.bfloat16), "dp").astype(jnp.float32)
    return (grad_x[None], grad_w.reshape(width_row, 3, width_col))


def swap(value, axis, step):
    size = lax.axis_size(axis)
    return lax.ppermute(value, axis, [(i, i ^ step) for i in range(size)])


LINE = (0, 2, 3, 1)


def along(value, steps):
    size = len(LINE)
    pairs = [(LINE[i], LINE[(i + steps) % size]) for i in range(size)]
    return lax.ppermute(value, "col", pairs)


def behind(z, steps):
    for _ in range(steps):
        z = jnp.where(z < 2, 2 * z + 1, 2 * z - 4)
    return z


VMEM = pl.BlockSpec(memory_space=pltpu.VMEM)
SMEM = pl.BlockSpec(memory_space=pltpu.SMEM)
HBM = pl.BlockSpec(memory_space=pltpu.HBM)
ANY = pl.BlockSpec(memory_space=pl.ANY)


PER_MICRO = 1.1e9


def hbm(value):
    return pltpu.with_memory_space_constraint(value, pltpu.HBM)


def bf16(*shape):
    return jax.ShapeDtypeStruct(shape, jnp.bfloat16)


def local(
    me, body, outs, ins, micros, in_specs=None, scratch=(), out_specs=None, aliases=None, late=(), placed=True
):
    place, *turn = me
    first = [place] if placed else []
    late = [*turn, *late]
    n_in = len(first) + len(ins)

    def ordered(*refs):
        body(*refs[:n_in], *refs[n_in + len(late) + 1 :])

    turns = {n_in: 0} if turn else {}
    moved = {len(first) + i: 1 + o for i, o in (aliases or {}).items()}
    turn, *results = pl.pallas_call(
        ordered,
        out_shape=[jax.ShapeDtypeStruct((8, LANES), jnp.float32), *outs],
        in_specs=[SMEM] * len(first) + [*(in_specs or [VMEM] * len(ins)), *[ANY] * len(late)],
        out_specs=[ANY, *(out_specs or [VMEM] * len(outs))],
        scratch_shapes=list(scratch),
        input_output_aliases={**turns, **moved},
        compiler_params=pltpu.CompilerParams(vmem_limit_bytes=16 * 2**20),
        cost_estimate=pl.CostEstimate(
            flops=int(micros * PER_MICRO), bytes_accessed=1, transcendentals=0
        ),
    )(*first, *ins, *late)
    return (place, turn), results


def multiply(x, w_ref, c, block_at, out_ref):
    block = out_ref.shape[-1]
    at = pl.multiple_of(block_at * block, LANES)
    out_ref[c] = jnp.dot(
        x, w_ref[c, :, pl.ds(at, block)], preferred_element_type=jnp.float32
    ).astype(jnp.bfloat16)


def begin(me, x, up, w, block):
    parts, depth, width = w.shape
    high = up.shape[0]

    def body(me_ref, x_hbm, up_hbm, w_hbm, *refs):
        w_ref, x_ref, there_ref, here_ref, across_ref, *away_refs, place_ref, up_ref, sems = refs
        row = me_ref[0]
        place_ref[0] = row
        place_ref[1] = me_ref[1]
        loads = [pltpu.make_async_copy(up_hbm, up_ref, sems.at[0])]
        loads += [pltpu.make_async_copy(x_hbm, x_ref, sems.at[1])]
        loads += [
            pltpu.make_async_copy(w_hbm.at[c], w_ref.at[c], sems.at[2 + c]) for c in range(parts)
        ]
        for load in loads:
            load.start()
        loads[0].wait()
        for j in range(2):
            at = pl.multiple_of((row ^ (2 * j + 1)) * block, LANES)
            there_ref[j] = up_ref[:, pl.ds(at, block)]
        here_ref[...] = up_ref[:, pl.ds(pl.multiple_of(row * block, LANES), block)]
        across_ref[...] = up_ref[:, pl.ds(pl.multiple_of((row ^ 2) * block, LANES), block)]
        loads[1].wait()
        for c in range(parts):
            loads[2 + c].wait()
            for j in range(2):
                multiply(x_ref[...], w_ref, c, row ^ (2 * j + 1), away_refs[j])

    return local(
        me,
        body,
        [
            pltpu.VMEM(w.shape, w.dtype),
            pltpu.VMEM(x.shape, x.dtype),
            bf16(2, high, block),
            bf16(high, block),
            bf16(high, block),
            bf16(parts, high, block),
            bf16(parts, high, block),
            pltpu.SMEM((2,), jnp.int32),
        ],
        [hbm(x), hbm(up), hbm(w)],
        3.5,
        [HBM, HBM, HBM],
        out_specs=[VMEM] * 7 + [SMEM],
        scratch=[
            pltpu.VMEM(up.shape, up.dtype),
            pltpu.SemaphoreType.DMA((2 + parts,)),
        ],
    )


def project(me, xs, w, block, other, late=()):
    parts = w.shape[0]
    tall = xs[0].shape[0] * len(xs)

    def body(me_ref, *refs):
        w_ref, out_refs = refs[len(xs)], refs[len(xs) + 1 :]
        x = jnp.concatenate([x[...] for x in refs[: len(xs)]], axis=0)
        for j in (1, 0):
            for c in range(parts):
                multiply(x, w_ref, c, me_ref[0] ^ (2 * j + other), out_refs[j])

    outs = [bf16(parts, tall, block)] * 2
    return local(me, body, outs, [*xs, w], 2.0 * len(xs), late=late)


def laid_out(me, groups, ups, late=()):
    parts, _, block = groups[0][2].shape
    tokens = sum(far.shape[1] for _, _, far in groups)
    high = ups[0].shape[0]
    n_in = 3 * len(groups)

    def body(me_ref, *refs):
        ins, up_refs, (seq, cot) = refs[:n_in], refs[n_in:-2], refs[-2:]
        row, z = me_ref[0], me_ref[1]
        for at in (0, PAD + tokens):
            seq[:, at : at + PAD, :] = jnp.zeros((parts, PAD, block), jnp.float32)
            cot[at : at + PAD, :] = jnp.zeros((PAD, block), jnp.float32)
        for s in range(len(groups)):
            keep, near, far = ins[3 * s : 3 * s + 3]
            to = pl.multiple_of(behind(z, s) * high + PAD, PAD)
            for c in range(parts):
                total = keep[c].astype(jnp.float32) + near[c].astype(jnp.float32)
                total = total + far[c].astype(jnp.float32)
                seq[c, pl.ds(to, high), :] = total.astype(jnp.bfloat16).astype(jnp.float32)
        for i, up in enumerate(up_refs):
            to = pl.multiple_of((row ^ i) * high + PAD, PAD)
            cot[pl.ds(to, high), :] = up[...].astype(jnp.float32)

    operands = [a for group in groups for a in group] + list(ups)
    outs = [
        pltpu.VMEM((parts, tokens + 2 * PAD, block), jnp.float32),
        pltpu.VMEM((tokens + 2 * PAD, block), jnp.float32),
    ]
    return local(me, body, outs, operands, 0.6, late=late)


def gate(me, seq, cot, feature_taps, inner_taps, high, shards, one=None, late=()):
    lags, parts, _ = feature_taps.shape
    long_lags = inner_taps.shape[0]
    block = cot.shape[1]
    window = high + 2 * PAD
    ins = [seq, cot, feature_taps, inner_taps] + ([] if one is None else [one])

    def back(value, lag):
        return pltpu.roll(value, lag, 0) if lag else value

    def ahead(value, lag):
        return pltpu.roll(value, window - lag, 0) if lag else value

    def body(me_ref, seq_ref, cot_ref, taps_ref, long_ref, *refs):
        row, z = me_ref[0], me_ref[1]
        if one is not None:
            one_ref, all_ref, last_ref, two_ref = refs
            all_ref[0] = one_ref[...]

        @pl.loop(0, block // LANES)
        def _(half):
            lanes = pl.ds(pl.multiple_of(half * LANES, LANES), LANES)
            wide = pl.ds(pl.multiple_of(row * block + half * LANES, LANES), LANES)
            taps = [[taps_ref[s, c : c + 1, wide] for c in range(parts)] for s in range(lags)]
            long_taps = [long_ref[s : s + 1, wide] for s in range(long_lags)]
            for s in shards:
                rows = pl.ds(pl.multiple_of(behind(z, s) * high, PAD), window)
                mixed = []
                for c in range(parts):
                    proj = seq_ref[c, rows, lanes]
                    total = taps[0][c] * proj
                    for lag in range(1, lags):
                        total = total + taps[lag][c] * back(proj, lag)
                    mixed.append(total)
                query, key, value = mixed
                upstream = cot_ref[rows, lanes]
                product = (key * value).astype(jnp.bfloat16).astype(jnp.float32)
                inner = long_taps[0] * product
                for lag in range(1, long_lags):
                    inner = inner + long_taps[lag] * back(product, lag)
                grad_inner = upstream * query
                grad_product = long_taps[0] * grad_inner
                for lag in range(1, long_lags):
                    grad_product = grad_product + long_taps[lag] * ahead(grad_inner, lag)
                grads = (upstream * inner, grad_product * value, grad_product * key)
                for c, grad in enumerate(grads):
                    total = taps[0][c] * grad
                    for lag in range(1, lags):
                        total = total + taps[lag][c] * ahead(grad, lag)
                    done = total[PAD : PAD + high].astype(jnp.bfloat16)
                    if one is None:
                        refs[0][c, :, lanes] = done
                        continue
                    all_ref[(s - 1) % 4, c, :, lanes] = done
                    if s == 2:
                        two_ref[c, :, lanes] = done
                    else:
                        last_ref[(s - 3) % 4, c, :, lanes] = done

    single = (parts, high, block)
    outs = [bf16(*single)]
    if one is not None:
        outs = [bf16(4, *single), bf16(2, *single), *outs]
    return local(me, body, outs, ins, 0.8 * len(shards), late=late)


def relay(me, *values, late=()):
    return local(
        me,
        lambda *refs: None,
        [jax.ShapeDtypeStruct(value.shape, value.dtype) for value in values],
        values,
        0.01,
        [ANY] * len(values),
        out_specs=[ANY] * len(values),
        aliases={i: i for i in range(len(values))},
        late=late,
        placed=False,
    )


def input_grads(me, pieces, w, late=()):
    parts, depth, width = w.shape
    high, block = pieces[0][0].shape[-2:]
    shards = len(pieces[0][1])

    def body(me_ref, *refs):
        w_ref, outs, wide = refs[len(pieces)], refs[len(pieces) + 1 : -1], refs[-1]
        for i, (g, (_, which)) in enumerate(zip(refs, pieces)):
            at = pl.multiple_of((me_ref[0] ^ i) * block, LANES)
            for s, index in enumerate(which):
                shard = g if index is None else g.at[index]
                wide[:, s * high : (s + 1) * high, pl.ds(at, block)] = shard[...]
        total = None
        for c in range(parts):
            term = lax.dot_general(
                wide[c], w_ref[c], (((1,), (1,)), ((), ())), preferred_element_type=jnp.float32
            )
            total = term if total is None else total + term
        for s, out in enumerate(outs):
            out[...] = total[s * high : (s + 1) * high].astype(jnp.bfloat16)

    return local(
        me,
        body,
        [bf16(high, depth)] * shards,
        [*(g for g, _ in pieces), w],
        6.0 if shards > 1 else 0.8,
        scratch=[pltpu.VMEM((parts, shards * high, width), jnp.bfloat16)],
        late=late,
    )


def turned(me, xs, late=()):
    high, depth = xs[0].shape

    def body(*refs):
        for s, x in enumerate(refs[:-1]):
            refs[-1][:, s * high : (s + 1) * high] = x[...].T

    me, (out,) = local(me, body, [bf16(depth, high * len(xs))], xs, 0.1 * len(xs), late=late, placed=False)
    return me, out


def weight_grads(me, done, xts, blocks, width, begun=None, final=True):
    depth = xts[0].shape[0]
    flat = [p for _, pieces in blocks for p in pieces]
    parts, high, block = flat[0][0].shape[-3:]
    unique = []
    for g, _ in flat:
        if not any(g is u for u in unique):
            unique.append(g)
    spot = {id(u): n for n, u in enumerate(unique)}
    tokens = high * len(blocks[0][1])
    wide = block * len(blocks)
    cuts, spare = 4, 4
    tall = depth // cuts
    n_in = len(xts) + len(unique) + (begun is not None) + (done is not None)

    def body(me_ref, *refs):
        x_refs, g_refs = refs[: len(xts)], refs[len(xts) : n_in]
        out_ref, xt, gs, *rest = refs[n_in:]
        at = 0
        for x in x_refs:
            xt[:, at : at + x.shape[1]] = x[...]
            at += x.shape[1]
        row = me_ref[0]
        start = pl.multiple_of((row ^ blocks[0][0]) // CORES * wide, wide)
        copies = []
        for c in range(parts):
            for i, pieces in blocks:
                lanes = pl.ds(pl.multiple_of((row ^ i) % CORES * block, LANES), block)
                for k, (g, index) in enumerate(pieces):
                    g_ref = g_refs[spot[id(g)]]
                    shard = g_ref if index is None else g_ref.at[index]
                    gs[c % 2, k * high : (k + 1) * high, lanes] = shard[c]
            for m in range(cuts):
                rows = pl.ds(m * tall, tall)
                part = jnp.dot(xt[rows, :], gs[c % 2], preferred_element_type=jnp.float32)
                if begun is not None:
                    part = part + g_refs[len(unique)][c, rows, :]
                if not final:
                    out_ref[c, rows, :] = part
                    continue
                held, sems = rest
                slot = len(copies) % spare
                if len(copies) >= spare:
                    copies[-spare].wait()
                held[slot] = part
                copies.append(
                    pltpu.make_async_copy(
                        held.at[slot], out_ref.at[c, rows, pl.ds(start, wide)], sems.at[slot]
                    )
                )
                copies[-1].start()
        for copy in copies[-spare:]:
            copy.wait()

    ins = [*xts, *unique] + ([] if begun is None else [begun])
    specs = [VMEM] * len(ins)
    aliases = {}
    if done is not None:
        aliases = {len(ins): 0}
        ins.append(done)
        specs.append(ANY)
    scratch = [
        pltpu.VMEM((depth, tokens), jnp.bfloat16),
        pltpu.VMEM((2, tokens, wide), jnp.bfloat16),
    ]
    out = pltpu.VMEM((parts, depth, wide), jnp.float32)
    if final:
        out = jax.ShapeDtypeStruct((parts, depth, width), jnp.float32)
        scratch += [
            pltpu.VMEM((spare, tall, wide), jnp.float32),
            pltpu.SemaphoreType.DMA((spare,)),
        ]
    me, (out,) = local(
        me,
        body,
        [out],
        ins,
        6.0 if final else 4.0,
        specs,
        scratch=scratch,
        out_specs=[ANY if final else VMEM],
        aliases=aliases,
    )
    return me, out


def total(me, terms, late=()):
    def body(*refs):
        acc = refs[0][...].astype(jnp.float32)
        for ref in refs[1:-1]:
            acc = acc + ref[...].astype(jnp.float32)
        refs[-1][...] = acc.astype(jnp.bfloat16)

    me, (out,) = local(me, body, [bf16(*terms[0].shape)], terms, 0.05, late=late, placed=False)
    return me, out


def by_channels(inputs, weights, feature_taps, inner_taps, grad_out):
    x_own = inputs[0]
    block = weights.shape[2] // lax.axis_size("row")
    width = weights.shape[2]
    me = (jnp.stack([lax.axis_index("row"), lax.axis_index("col")]).astype(jnp.int32),)

    def send(name, value, axis, step):
        with jax.named_scope(name):
            return along(value, step) if axis == "col" else swap(value, axis, step)

    x1 = send("x1", x_own, "col", 1)
    x2 = send("x2", x1, "col", 1)
    x3 = send("x3", x2, "col", 1)
    with jax.named_scope("begin"):
        me, (w, x_own, there, here, across, *away, place) = begin(
            me, x_own, grad_out[0], jnp.transpose(weights, (1, 0, 2)), block
        )
    me = (place, *me[1:])
    def spread(me, name, x, away, turn=(), late=()):
        got = [send(name + "_core%d" % j, away[j], "row", 1) for j in range(2)]
        with jax.named_scope(name + "_keep"):
            me, keep = project(me, [x], w, block, 0)
        with jax.named_scope(name + "_join"):
            me, both = total(me, [keep[1], got[1]], [got[0]])
        groups.append((keep[0], got[0], send(name + "_y", both, "row", CORES)))
        if turn:
            with jax.named_scope(name + "_turned"):
                me, xt = turned(me, turn, late)
            xts.append(xt)
            others.append(send(name + "_xt_x", xt, "dp", 1))
        return me

    groups, xts, others = [], [], []
    me = spread(me, "proj0", x_own, away)
    with jax.named_scope("proj1_away"):
        me, away = project(me, [x1], w, block, 1)
    me = spread(me, "proj1", x1, away, [x_own, x1], [groups[0][2]])
    with jax.named_scope("proj2_away"):
        me, away = project(me, [x2], w, block, 1)
    me = spread(me, "proj2", x2, away, [x2], [groups[1][2]])
    with jax.named_scope("relay_up"):
        me, (there,) = relay(me, there)
    near = send("up_core", there, "row", 1)
    far = send("up_y", jnp.stack([across, near[1]]), "row", CORES)
    ups = [here, near[0], far[0], far[1]]
    with jax.named_scope("proj3_away"):
        me, away = project(me, [x3], w, block, 1)
    me = spread(me, "proj3", x3, away, [x3], [groups[2][2], others[0]])
    with jax.named_scope("laid_out"):
        me, (seq, cot) = laid_out(me, groups, ups)
    high = x_own.shape[0]
    with jax.named_scope("gate1"):
        me, (g1,) = gate(me, seq, cot, feature_taps, inner_taps, high, (1,), late=others[1:2])
    y1 = send("g1_y", g1, "row", CORES)
    c1 = send("g1_core", g1, "row", 1)
    with jax.named_scope("gate230"):
        me, (g, g30, g2) = gate(me, seq, cot, feature_taps, inner_taps, high, (2, 3, 0), g1)
    c2, c30 = send("g2_core", g2, "row", 1), send("g30_core", g30, "row", 1)
    with jax.named_scope("relay_g2"):
        me, (g2,) = relay(me, g2, late=[y1, *others[2:]])
    y2 = send("g2_y", g2, "row", CORES)
    x = send("g_x", g, "dp", 1)
    cy1, cy2 = send("gy1_core", y1, "row", 1), send("gy2_core", y2, "row", 1)
    with jax.named_scope("input_grads1"):
        pieces = [(g, [0]), (c1, [None]), (y1, [None]), (cy1, [None])]
        me, (share1,) = input_grads(me, pieces, w)
    passed = send("share1", share1, "col", 1)
    with jax.named_scope("relay_g30"):
        me, (g30,) = relay(me, g30)
    y30 = send("g30_y", g30, "row", CORES)

    def whole(a):
        return [(a, 3), (a, 0), (a, 1), (a, 2)]

    def cut(last, one, two):
        return [(last, 1), (one, None), (two, None), (last, 0)]

    def halves(low, high):
        return [(high, 1), (low, 0), (low, 1), (high, 0)]

    with jax.named_scope("weight_grads_near_own"):
        blocks = [(0, whole(g)), (1, cut(c30, c1, c2))]
        me, begun = weight_grads(me, None, xts, blocks, width, final=False)
    with jax.named_scope("input_grads2"):
        pieces = [(g, [1]), (c2, [None]), (y2, [None]), (cy2, [None])]
        me, (share2,) = input_grads(me, pieces, w)
    with jax.named_scope("total2"):
        me, share2 = total(me, [share2, passed])
    passed = send("share2", share2, "col", 1)
    with jax.named_scope("relay_x"):
        me, (x,) = relay(me, x)
    xy12, cx = send("gx12_y", x[:2], "row", CORES), send("gx_core", x, "row", 1)
    with jax.named_scope("relay_y30"):
        me, (y30,) = relay(me, y30)
    xy30, cy30 = send("gy30_x", y30, "dp", 1), send("gy30_core", y30, "row", 1)
    with jax.named_scope("input_grads30"):
        pieces = [(g, [2, 3]), (c30, [0, 1]), (y30, [0, 1]), (cy30, [0, 1])]
        me, (share3, share0) = input_grads(me, pieces, w)
    with jax.named_scope("weight_grads_near"):
        blocks = [(0, whole(x)), (1, whole(cx))]
        me, grad_w = weight_grads(me, None, others, blocks, width, begun)
    with jax.named_scope("total3"):
        me, share3 = total(me, [share3, passed])
    passed = send("share3", share3, "col", 1)
    with jax.named_scope("relay_xy"):
        me, (xy12, xy30) = relay(me, xy12, xy30)
    cxy12, cxy30 = send("gxy12_core", xy12, "row", 1), send("gxy30_core", xy30, "row", 1)
    with jax.named_scope("weight_grads_far"):
        blocks = [
            (2, cut(y30, y1, y2) + halves(xy12, xy30)),
            (3, cut(cy30, cy1, cy2) + halves(cxy12, cxy30)),
        ]
        me, grad_w = weight_grads(me, grad_w, xts + others, blocks, width)
    with jax.named_scope("total0"):
        me, grad_in = total(me, [share0, passed])
    return (grad_in[None], jnp.transpose(grad_w, (1, 0, 2)))


def solution(mesh):
    placed = (
        P("dp", "col", "row"),
        P("row", None, "col"),
        P(None, None, "col"),
        P(None, "col"),
        P("dp", "row", "col"),
    )

    def on_device(inputs, weights, feature_taps, inner_taps, grad_out):
        n_row = mesh.shape["row"]
        fits = weights.shape[2] % (n_row * LANES) == 0 and inputs.shape[1] % LANES == 0
        small = n_row == 2 * CORES and mesh.shape["dp"] == 2 and mesh.shape["col"] == 4
        plan = by_channels if fits and small else by_tokens
        return plan(inputs, weights, feature_taps, inner_taps, grad_out)

    return jax.shard_map(
        on_device,
        mesh=mesh,
        in_specs=placed,
        out_specs=(P("dp", "col", "row"), P("row", None, "col")),
        check_vma=False,
    )
```

profile of v0, /device:TPU:0, one launch (start us, length us, event | category | flops | bytes accessed | tf_op | source)
XLA Modules:
  0.0 88.7 jit_solution(12379572895403742863)
XLA Ops:
  0.6 4.1 %collective-permute-start.3 = (bf16[128,1024]{1,0:T(8,128)(2,1)}, bf16[128,1024]{1,0:T(8,128)(2,1)S(1)}, u32[]{:S(2)}, u32[]{:S(2)}) collective-permute-start(bf16[128,1024]{1,0:T(8,128)(2,1)} %bitcast.17), channel_id=1, source_target_pairs={{0,2},{2,3},{3,1},{1,0},{4,6},{6,7},{7,5},{5,4},{8,10},{10,11},{11... | collective-permute-start | bytes 786440 | tf_op jit(solution)/shard_map/x1/ppermute | solution.py:112
  4.8 4.0 %begin.1 = (f32[8,128]{1,0:T(8,128)S(1)}, bf16[3,1024,1024]{2,1,0:T(8,128)(2,1)S(1)}, bf16[128,1024]{1,0:T(8,128)(2,1)S(1)}, bf16[2,128,256]{2,1,0:T(8,128)(2,1)...) custom-call(s32[2]{0:T(128)S(1)} %pad_add_fusion.refs_0_, ...), custom_call_target="tpu_custom_call" | custom-call | flops 3849999872 | bytes 1 | tf_op jit(solution)/shard_map/begin/pallas_call | solution.py:151
  8.8 0.5 collective-permute-start.1
  9.3 0.6 proj0_keep.1
  10.0 0.3 collective-permute-done.refs_3_.refs_2_
  10.3 0.3 collective-permute-done.1.refs_1_
  10.6 1.6 %collective-permute-start.2 = (bf16[3,128,256]{2,1,0:T(8,128)(2,1)S(1)}, bf16[3,128,256]{2,1,0:T(8,128)(2,1)S(1)}, u32[]{:S(2)}, u32[]{:S(2)}) collective-permute-start(bf16[3,128,256]{2,1,0:T(8,128)(2,1)S(1)} %get-tuple-element.95), channel_id=1, source_target_pairs={{0,8},{4,12},{8,0},{12,4},{1,9},{5,13},{9,1},{13,5},{2,10},{6,14},... | collective-permute-start | bytes 589832 | tf_op jit(solution)/shard_map/proj0_y/ppermute | solution.py:103
  12.2 1.7 %collective-permute-start.7 = (bf16[128,1024]{1,0:T(8,128)(2,1)S(1)}, bf16[128,1024]{1,0:T(8,128)(2,1)S(1)}, u32[]{:S(2)}, u32[]{:S(2)}) collective-permute-start(bf16[128,1024]{1,0:T(8,128)(2,1)S(1)} %collective-permute-done.3.refs_1_), channel_id=1, source_target_pairs={{0,2},{2,3},{3,1},{1,0},{4,6},{6,7},{7,5},{5,4},{8,10},{10,11},{11... | collective-permute-start | bytes 786440 | tf_op jit(solution)/shard_map/x2/ppermute | solution.py:112
  13.9 0.6 proj1_away.1
  14.6 0.5 collective-permute-start.5
  15.1 0.6 proj1_keep.1
  15.7 0.3 collective-permute-done.4.refs_3_.refs_5_
  16.0 0.3 collective-permute-done.5.refs_1_
  16.3 1.6 %collective-permute-start.6 = (bf16[3,128,256]{2,1,0:T(8,128)(2,1)S(1)}, bf16[3,128,256]{2,1,0:T(8,128)(2,1)S(1)}, u32[]{:S(2)}, u32[]{:S(2)}) collective-permute-start(bf16[3,128,256]{2,1,0:T(8,128)(2,1)S(1)} %get-tuple-element.103), channel_id=1, source_target_pairs={{0,8},{4,12},{8,0},{12,4},{1,9},{5,13},{9,1},{13,5},{2,10},{6,14},... | collective-permute-start | bytes 589832 | tf_op jit(solution)/shard_map/proj1_y/ppermute | solution.py:103
  18.1 1.6 %collective-permute-start.17 = (bf16[1024,256]{1,0:T(8,128)(2,1)S(1)}, bf16[1024,256]{1,0:T(8,128)(2,1)S(1)}, u32[]{:S(2)}, u32[]{:S(2)}) collective-permute-start(bf16[1024,256]{1,0:T(8,128)(2,1)S(1)} %get-tuple-element.128.refs_1_), channel_id=1, source_target_pairs={{0,16},{16,0},{1,17},{17,1},{2,18},{18,2},{3,19},{19,3},{4,20},{20... | collective-permute-start | bytes 1572872 | tf_op jit(solution)/shard_map/proj1_xt_x/ppermute | solution.py:103
  19.7 0.7 collective-permute-done.7.refs_1_.refs_0_
  20.4 2.5 %collective-permute-start.11 = (bf16[128,1024]{1,0:T(8,128)(2,1)S(1)}, bf16[128,1024]{1,0:T(8,128)(2,1)S(1)}, u32[]{:S(2)}, u32[]{:S(2)}) collective-permute-start(bf16[128,1024]{1,0:T(8,128)(2,1)S(1)} %collective-permute-done.7.refs_1_.refs_0_), channel_id=1, source_target_pairs={{0,2},{2,3},{3,1},{1,0},{4,6},{6,7},{7,5},{5,4},{8,10},{10,11},{11... | collective-permute-start | bytes 786440 | tf_op jit(solution)/shard_map/x3/ppermute | solution.py:112
  22.8 0.6 proj2_away.1
  23.5 0.5 collective-permute-start.9
  24.0 0.6 proj2_keep.1
  24.6 0.3 collective-permute-done.8.refs_3_.refs_8_
  24.9 0.3 collective-permute-done.9.refs_1_
  25.4 0.3 collective-permute-start.15
  25.7 0.7 collective-permute-start.10
  26.4 1.3 %collective-permute-done.11.refs_1_.refs_0_ = bf16[128,1024]{1,0:T(8,128)(2,1)S(1)} collective-permute-done((bf16[128,1024]{1,0:T(8,128)(2,1)S(1)}, bf16[128,1024]{1,0:T(8,128)(2,1)S(1)}, u32[]{:S(2)}, u32[]{:S(2)}) %collective-permute-start.11) | collective-permute-done | bytes 262176 | tf_op jit(solution)/shard_map/x3/ppermute | solution.py:112
  27.7 0.6 proj3_away.1
  28.4 0.5 collective-permute-start.13
  28.9 0.7 collective-permute-start.16
  29.6 0.6 proj3_keep.1
  30.3 1.4 %collective-permute-start.18 = (bf16[1024,128]{1,0:T(8,128)(2,1)S(1)}, bf16[1024,128]{1,0:T(8,128)(2,1)S(1)}, u32[]{:S(2)}, u32[]{:S(2)}) collective-permute-start(bf16[1024,128]{1,0:T(8,128)(2,1)S(1)} %get-tuple-element.133.refs_2_), channel_id=1, source_target_pairs={{0,16},{16,0},{1,17},{17,1},{2,18},{18,2},{3,19},{19,3},{4,20},{20... | collective-permute-start | bytes 786440 | tf_op jit(solution)/shard_map/proj2_xt_x/ppermute | solution.py:103
  31.7 1.6 %collective-permute-start.14 = (bf16[3,128,256]{2,1,0:T(8,128)(2,1)S(1)}, bf16[3,128,256]{2,1,0:T(8,128)(2,1)S(1)}, u32[]{:S(2)}, u32[]{:S(2)}) collective-permute-start(bf16[3,128,256]{2,1,0:T(8,128)(2,1)S(1)} %get-tuple-element.123), channel_id=1, source_target_pairs={{0,8},{4,12},{8,0},{12,4},{1,9},{5,13},{9,1},{13,5},{2,10},{6,14},... | collective-permute-start | bytes 589832 | tf_op jit(solution)/shard_map/proj3_y/ppermute | solution.py:103
  33.3 3.0 %collective-permute-done.16 = bf16[2,128,256]{2,1,0:T(8,128)(2,1)S(1)} collective-permute-done((bf16[2,128,256]{2,1,0:T(8,128)(2,1)S(1)}, bf16[2,128,256]{2,1,0:T(8,128)(2,1)S(1)}, u32[]{:S(2)}, u32[]{:S(2)}) %collective-permute-start.16) | collective-permute-done | bytes 131104 | tf_op jit(solution)/shard_map/up_y/ppermute | solution.py:103
  36.4 1.6 %collective-permute-start.23 = (bf16[1024,128]{1,0:T(8,128)(2,1)S(1)}, bf16[1024,128]{1,0:T(8,128)(2,1)S(1)}, u32[]{:S(2)}, u32[]{:S(2)}) collective-permute-start(bf16[1024,128]{1,0:T(8,128)(2,1)S(1)} %get-tuple-element.140.refs_3_), channel_id=1, source_target_pairs={{0,16},{16,0},{1,17},{17,1},{2,18},{18,2},{3,19},{19,3},{4,20},{20... | collective-permute-start | bytes 786440 | tf_op jit(solution)/shard_map/proj3_xt_x/ppermute | solution.py:103
  38.0 1.9 %collective-permute-done.14.refs_12_ = bf16[3,128,256]{2,1,0:T(8,128)(2,1)S(1)} collective-permute-done((bf16[3,128,256]{2,1,0:T(8,128)(2,1)S(1)}, bf16[3,128,256]{2,1,0:T(8,128)(2,1)S(1)}, u32[]{:S(2)}, u32[]{:S(2)}) %collective-permute-start.14) | collective-permute-done | bytes 196640 | tf_op jit(solution)/shard_map/proj3_y/ppermute | solution.py:103
  39.8 0.4 laid_out.1
  40.2 0.6 gate1.1
  40.8 0.7 collective-permute-start.21
  41.5 1.7 %gate230.1 = (f32[8,128]{1,0:T(8,128)S(1)}, bf16[4,3,128,256]{3,2,1,0:T(8,128)(2,1)S(1)}, bf16[2,3,128,256]{3,2,1,0:T(8,128)(2,1)S(1)}, bf16[3,128,256]{2,1,0:T(8,128)(2,1)S(1)}) custom-call(s32[2]{0:T(128)S(4)} %get-tuple-element.86.refs_0_, f32[3,528,256]{2,1,0:T(8,128)S(1)} %get-tuple-element.130.refs_1_, ...), custom_call_target="tpu_custom_call", output_to_operand_aliasing={{0}: (6, {})} | custom-call | flops 2640000000 | bytes 1 | tf_op jit(solution)/shard_map/gate230/pallas_call | solution.py:151
  43.3 0.5 collective-permute-start.26
  43.7 1.5 %collective-permute-start.25 = (bf16[4,3,128,256]{3,2,1,0:T(8,128)(2,1)S(1)}, bf16[4,3,128,256]{3,2,1,0:T(8,128)(2,1)S(1)}, u32[]{:S(2)}, u32[]{:S(2)}) collective-permute-start(bf16[4,3,128,256]{3,2,1,0:T(8,128)(2,1)S(1)} %get-tuple-element.136.refs_1_.refs_4_), channel_id=1, source_target_pairs={{0,16},{16,0},{1,17},{17,1},{2,18},{18,2},{3,19},{19,3},{4,20},{20... | collective-permute-start | bytes 2359304 | tf_op jit(solution)/shard_map/g_x/ppermute | solution.py:103
  45.2 1.9 %collective-permute-done.21.refs_2_.refs_3_.refs_8_ = bf16[3,128,256]{2,1,0:T(8,128)(2,1)S(1)} collective-permute-done((bf16[3,128,256]{2,1,0:T(8,128)(2,1)S(1)}, bf16[3,128,256]{2,1,0:T(8,128)(2,1)S(1)}, u32[]{:S(2)}, u32[]{:S(2)}) %collective-permute-start.21) | collective-permute-done | bytes 196640 | tf_op jit(solution)/shard_map/g1_y/ppermute | solution.py:103
  47.1 0.7 collective-permute-start.27
  47.9 0.7 collective-permute-done.22.refs_4_.refs_13_
  48.6 2.2 %input_grads1.1 = (f32[8,128]{1,0:T(8,128)S(1)}, bf16[128,1024]{1,0:T(8,128)(2,1)S(1)}) custom-call(s32[2]{0:T(128)S(4)} %get-tuple-element.86.refs_0_, bf16[4,3,128,256]{3,2,1,0:T(8,128)(2,1)S(1)} %get-tuple-element.136.refs_1_.refs_4_, bf16[3,128,256]{2,1,0:T(8,128)(2,1)S(1)} %collective-permute-done.20.refs_2_.refs_6_, ...), custom_call_target="tpu_custom_call", output_to_operand_aliasing={{0}: (6, {})} | custom-call | flops 880000000 | bytes 1 | tf_op jit(solution)/shard_map/input_grads1/pallas_call | solution.py:151
  50.8 2.4 %collective-permute-start.29 = (bf16[128,1024]{1,0:T(8,128)(2,1)S(1)}, bf16[128,1024]{1,0:T(8,128)(2,1)S(1)}, u32[]{:S(2)}, u32[]{:S(2)}) collective-permute-start(bf16[128,1024]{1,0:T(8,128)(2,1)S(1)} %get-tuple-element.148), channel_id=1, source_target_pairs={{0,2},{2,3},{3,1},{1,0},{4,6},{6,7},{7,5},{5,4},{8,10},{10,11},{11... | collective-permute-start | bytes 786440 | tf_op jit(solution)/shard_map/share1/ppermute | solution.py:112
  53.2 1.1 %collective-permute-start.24 = (bf16[2,3,128,256]{3,2,1,0:T(8,128)(2,1)S(1)}, bf16[2,3,128,256]{3,2,1,0:T(8,128)(2,1)S(1)}, u32[]{:S(2)}, u32[]{:S(2)}) collective-permute-start(bf16[2,3,128,256]{3,2,1,0:T(8,128)(2,1)S(1)} %get-tuple-element.143), channel_id=1, source_target_pairs={{0,8},{4,12},{8,0},{12,4},{1,9},{5,13},{9,1},{13,5},{2,10},{6,14},... | collective-permute-start | bytes 1179656 | tf_op jit(solution)/shard_map/g30_y/ppermute | solution.py:103
  54.5 2.0 %weight_grads_near_own.1 = (f32[8,128]{1,0:T(8,128)S(1)}, f32[3,1024,512]{2,1,0:T(8,128)S(1)}) custom-call(s32[2]{0:T(128)S(4)} %get-tuple-element.86.refs_0_, bf16[1024,256]{1,0:T(8,128)(2,1)S(1)} %get-tuple-element.128.refs_1_, bf16[1024,128]{1,0:T(8,128)(2,1)S(1)} %get-tuple-element.133.refs_2_, ...), custom_call_target="tpu_custom_call", output_to_operand_aliasing={{0}: (8, {})} | custom-call | flops 4400000000 | bytes 1 | tf_op jit(solution)/shard_map/weight_grads_near_own/pallas_call | solution.py:151
  56.5 2.2 %input_grads2.1 = (f32[8,128]{1,0:T(8,128)S(1)}, bf16[128,1024]{1,0:T(8,128)(2,1)S(1)}) custom-call(s32[2]{0:T(128)S(4)} %get-tuple-element.86.refs_0_, bf16[4,3,128,256]{3,2,1,0:T(8,128)(2,1)S(1)} %get-tuple-element.136.refs_1_.refs_4_, bf16[3,128,256]{2,1,0:T(8,128)(2,1)S(1)} %collective-permute-done.26.refs_7_.refs_2_, ...), custom_call_target="tpu_custom_call", output_to_operand_aliasing={{0}: (6, {})} | custom-call | flops 880000000 | bytes 1 | tf_op jit(solution)/shard_map/input_grads2/pallas_call | solution.py:151
  58.7 0.7 collective-permute-done.29.refs_1_
  59.5 3.8 %collective-permute-done.25.refs_0_ = bf16[4,3,128,256]{3,2,1,0:T(8,128)(2,1)S(1)} collective-permute-done((bf16[4,3,128,256]{3,2,1,0:T(8,128)(2,1)S(1)}, bf16[4,3,128,256]{3,2,1,0:T(8,128)(2,1)S(1)}, u32[]{:S(2)}, u32[]{:S(2)}) %collective-permute-start.25) | collective-permute-done | bytes 786464 | tf_op jit(solution)/shard_map/g_x/ppermute | solution.py:103
  63.3 0.8 collective-permute-done.24.refs_0_
  64.1 0.5 collective-permute-start.32
  64.6 2.4 %collective-permute-start.31 = (bf16[128,1024]{1,0:T(8,128)(2,1)S(1)}, bf16[128,1024]{1,0:T(8,128)(2,1)S(1)}, u32[]{:S(2)}, u32[]{:S(2)}) collective-permute-start(bf16[128,1024]{1,0:T(8,128)(2,1)S(1)} %get-tuple-element.156), channel_id=1, source_target_pairs={{0,2},{2,3},{3,1},{1,0},{4,6},{6,7},{7,5},{5,4},{8,10},{10,11},{11... | collective-permute-start | bytes 786440 | tf_op jit(solution)/shard_map/share2/ppermute | solution.py:112
  67.1 1.6 %collective-permute-start.35 = (bf16[2,3,128,256]{3,2,1,0:T(8,128)(2,1)S(1)}, bf16[2,3,128,256]{3,2,1,0:T(8,128)(2,1)S(1)}, u32[]{:S(2)}, u32[]{:S(2)}) collective-permute-start(bf16[2,3,128,256]{3,2,1,0:T(8,128)(2,1)S(1)} %get-tuple-element.152.refs_3_.refs_7_), channel_id=1, source_target_pairs={{0,16},{16,0},{1,17},{17,1},{2,18},{18,2},{3,19},{19,3},{4,20},{20... | collective-permute-start | bytes 1179656 | tf_op jit(solution)/shard_map/gy30_x/ppermute | solution.py:103
  68.8 2.0 %input_grads30.1 = (f32[8,128]{1,0:T(8,128)S(1)}, bf16[128,1024]{1,0:T(8,128)(2,1)S(1)}, bf16[128,1024]{1,0:T(8,128)(2,1)S(1)}) custom-call(s32[2]{0:T(128)S(4)} %get-tuple-element.86.refs_0_, bf16[4,3,128,256]{3,2,1,0:T(8,128)(2,1)S(1)} %get-tuple-element.136.refs_1_.refs_4_, ...), custom_call_target="tpu_custom_call", output_to_operand_aliasing={{0}: (6, {})} | custom-call | flops 6600000000 | bytes 1 | tf_op jit(solution)/shard_map/input_grads30/pallas_call | solution.py:151
  70.9 4.5 %weight_grads_near.1 = (f32[8,128]{1,0:T(8,128)S(1)}, f32[3,1024,1024]{2,1,0:T(8,128)}) custom-call(s32[2]{0:T(128)S(4)} %get-tuple-element.86.refs_0_, bf16[1024,256]{1,0:T(8,128)(2,1)S(1)} %collective-permute-done.17.refs_3_.refs_1_.refs_4_, bf16[1024,128]{1,0:T(8,128)(2,1)S(1)} %collective-permute-done.18.refs_6_.refs_2_.refs_5_, ...), custom_call_target="tpu_custom_call", output_to_operand_aliasing={{0}: (7, {})} | custom-call | flops 6600000000 | bytes 1 | tf_op jit(solution)/shard_map/weight_grads_near/pallas_call | solution.py:151
  75.4 3.8 %collective-permute-done.34.refs_0_ = bf16[2,3,128,256]{3,2,1,0:T(8,128)(2,1)S(1)} collective-permute-done((bf16[2,3,128,256]{3,2,1,0:T(8,128)(2,1)S(1)}, bf16[2,3,128,256]{3,2,1,0:T(8,128)(2,1)S(1)}, u32[]{:S(2)}, u32[]{:S(2)}) %collective-permute-start.34) | collective-permute-done | bytes 393248 | tf_op jit(solution)/shard_map/gx12_y/ppermute | solution.py:103
  79.2 0.5 collective-permute-start.37
  79.7 0.3 collective-permute-start.33
  80.0 0.9 %collective-permute-done.36.refs_15_ = bf16[2,3,128,256]{3,2,1,0:T(8,128)(2,1)S(1)} collective-permute-done((bf16[2,3,128,256]{3,2,1,0:T(8,128)(2,1)S(1)}, bf16[2,3,128,256]{3,2,1,0:T(8,128)(2,1)S(1)}, u32[]{:S(2)}, u32[]{:S(2)}) %collective-permute-start.36) | collective-permute-done | bytes 393248 | tf_op jit(solution)/shard_map/gxy30_core/ppermute | solution.py:103
  80.9 0.6 collective-permute-done.37.refs_16_
  81.5 6.0 %weight_grads_far.1 = (f32[8,128]{1,0:T(8,128)S(1)}, f32[3,1024,1024]{2,1,0:T(8,128)}) custom-call(s32[2]{0:T(128)S(4)} %get-tuple-element.86.refs_0_, bf16[1024,256]{1,0:T(8,128)(2,1)S(1)} %get-tuple-element.128.refs_1_, bf16[1024,128]{1,0:T(8,128)(2,1)S(1)} %get-tuple-element.133.refs_2_, ...), custom_call_target="tpu_custom_call", output_to_operand_aliasing={{0}: (18, {}), {1}: (17, {})} | custom-call | flops 6600000000 | bytes 1 | tf_op jit(solution)/shard_map/weight_grads_far/pallas_call | solution.py:151
  87.5 0.4 collective-permute-done.33.refs_1_
  88.0 0.8 total0.1
  (54 shorter events, 1.6 us)
Async XLA Ops:
  0.6 11.6 %collective-permute-start.3 = (bf16[128,1024]{1,0:T(8,128)(2,1)}, bf16[128,1024]{1,0:T(8,128)(2,1)S(1)}, u32[]{:S(2)}, u32[]{:S(2)}) collective-permute-start(bf16[128,1024]{1,0:T(8,128)(2,1)} %bitcast.17), channel_id=1, source_target_pairs={{0,2},{2,3},{3,1},{1,0},{4,6},{6,7},{7,5},{5,4},{8,10},{10,11},{11... | collective-permute-start | bytes 786440 | tf_op jit(solution)/shard_map/x1/ppermute | solution.py:112
  8.8 1.5 %collective-permute-start = (bf16[3,128,256]{2,1,0:T(8,128)(2,1)S(1)}, bf16[3,128,256]{2,1,0:T(8,128)(2,1)S(1)}, u32[]{:S(2)}, u32[]{:S(2)}) collective-permute-start(bf16[3,128,256]{2,1,0:T(8,128)(2,1)S(1)} %get-tuple-element.91), channel_id=1, source_target_pairs={{0,4},{4,0},{8,12},{12,8},{1,5},{5,1},{9,13},{13,9},{2,6},{6,2},{1... | collective-permute-start | bytes 589832 | tf_op jit(solution)/shard_map/proj0_core0/ppermute | solution.py:103
  8.8 1.7 %collective-permute-start.1 = (bf16[3,128,256]{2,1,0:T(8,128)(2,1)S(1)}, bf16[3,128,256]{2,1,0:T(8,128)(2,1)S(1)}, u32[]{:S(2)}, u32[]{:S(2)}) collective-permute-start(bf16[3,128,256]{2,1,0:T(8,128)(2,1)S(1)} %get-tuple-element.93), channel_id=1, source_target_pairs={{0,4},{4,0},{8,12},{12,8},{1,5},{5,1},{9,13},{13,9},{2,6},{6,2},{1... | collective-permute-start | bytes 589832 | tf_op jit(solution)/shard_map/proj0_core1/ppermute | solution.py:103
  10.6 7.3 %collective-permute-start.2 = (bf16[3,128,256]{2,1,0:T(8,128)(2,1)S(1)}, bf16[3,128,256]{2,1,0:T(8,128)(2,1)S(1)}, u32[]{:S(2)}, u32[]{:S(2)}) collective-permute-start(bf16[3,128,256]{2,1,0:T(8,128)(2,1)S(1)} %get-tuple-element.95), channel_id=1, source_target_pairs={{0,8},{4,12},{8,0},{12,4},{1,9},{5,13},{9,1},{13,5},{2,10},{6,14},... | collective-permute-start | bytes 589832 | tf_op jit(solution)/shard_map/proj0_y/ppermute | solution.py:103
  12.2 8.2 %collective-permute-start.7 = (bf16[128,1024]{1,0:T(8,128)(2,1)S(1)}, bf16[128,1024]{1,0:T(8,128)(2,1)S(1)}, u32[]{:S(2)}, u32[]{:S(2)}) collective-permute-start(bf16[128,1024]{1,0:T(8,128)(2,1)S(1)} %collective-permute-done.3.refs_1_), channel_id=1, source_target_pairs={{0,2},{2,3},{3,1},{1,0},{4,6},{6,7},{7,5},{5,4},{8,10},{10,11},{11... | collective-permute-start | bytes 786440 | tf_op jit(solution)/shard_map/x2/ppermute | solution.py:112
  14.5 1.5 %collective-permute-start.4 = (bf16[3,128,256]{2,1,0:T(8,128)(2,1)S(1)}, bf16[3,128,256]{2,1,0:T(8,128)(2,1)S(1)}, u32[]{:S(2)}, u32[]{:S(2)}) collective-permute-start(bf16[3,128,256]{2,1,0:T(8,128)(2,1)S(1)} %get-tuple-element.99), channel_id=1, source_target_pairs={{0,4},{4,0},{8,12},{12,8},{1,5},{5,1},{9,13},{13,9},{2,6},{6,2},{1... | collective-permute-start | bytes 589832 | tf_op jit(solution)/shard_map/proj1_core0/ppermute | solution.py:103
  14.6 1.7 %collective-permute-start.5 = (bf16[3,128,256]{2,1,0:T(8,128)(2,1)S(1)}, bf16[3,128,256]{2,1,0:T(8,128)(2,1)S(1)}, u32[]{:S(2)}, u32[]{:S(2)}) collective-permute-start(bf16[3,128,256]{2,1,0:T(8,128)(2,1)S(1)} %get-tuple-element.101), channel_id=1, source_target_pairs={{0,4},{4,0},{8,12},{12,8},{1,5},{5,1},{9,13},{13,9},{2,6},{6,2},{1... | collective-permute-start | bytes 589832 | tf_op jit(solution)/shard_map/proj1_core1/ppermute | solution.py:103
  16.3 9.0 %collective-permute-start.6 = (bf16[3,128,256]{2,1,0:T(8,128)(2,1)S(1)}, bf16[3,128,256]{2,1,0:T(8,128)(2,1)S(1)}, u32[]{:S(2)}, u32[]{:S(2)}) collective-permute-start(bf16[3,128,256]{2,1,0:T(8,128)(2,1)S(1)} %get-tuple-element.103), channel_id=1, source_target_pairs={{0,8},{4,12},{8,0},{12,4},{1,9},{5,13},{9,1},{13,5},{2,10},{6,14},... | collective-permute-start | bytes 589832 | tf_op jit(solution)/shard_map/proj1_y/ppermute | solution.py:103
  18.1 18.2 %collective-permute-start.17 = (bf16[1024,256]{1,0:T(8,128)(2,1)S(1)}, bf16[1024,256]{1,0:T(8,128)(2,1)S(1)}, u32[]{:S(2)}, u32[]{:S(2)}) collective-permute-start(bf16[1024,256]{1,0:T(8,128)(2,1)S(1)} %get-tuple-element.128.refs_1_), channel_id=1, source_target_pairs={{0,16},{16,0},{1,17},{17,1},{2,18},{18,2},{3,19},{19,3},{4,20},{20... | collective-permute-start | bytes 1572872 | tf_op jit(solution)/shard_map/proj1_xt_x/ppermute | solution.py:103
  20.4 7.3 %collective-permute-start.11 = (bf16[128,1024]{1,0:T(8,128)(2,1)S(1)}, bf16[128,1024]{1,0:T(8,128)(2,1)S(1)}, u32[]{:S(2)}, u32[]{:S(2)}) collective-permute-start(bf16[128,1024]{1,0:T(8,128)(2,1)S(1)} %collective-permute-done.7.refs_1_.refs_0_), channel_id=1, source_target_pairs={{0,2},{2,3},{3,1},{1,0},{4,6},{6,7},{7,5},{5,4},{8,10},{10,11},{11... | collective-permute-start | bytes 786440 | tf_op jit(solution)/shard_map/x3/ppermute | solution.py:112
  23.4 1.5 %collective-permute-start.8 = (bf16[3,128,256]{2,1,0:T(8,128)(2,1)S(1)}, bf16[3,128,256]{2,1,0:T(8,128)(2,1)S(1)}, u32[]{:S(2)}, u32[]{:S(2)}) collective-permute-start(bf16[3,128,256]{2,1,0:T(8,128)(2,1)S(1)} %get-tuple-element.108), channel_id=1, source_target_pairs={{0,4},{4,0},{8,12},{12,8},{1,5},{5,1},{9,13},{13,9},{2,6},{6,2},{1... | collective-permute-start | bytes 589832 | tf_op jit(solution)/shard_map/proj2_core0/ppermute | solution.py:103
  23.5 1.7 %collective-permute-start.9 = (bf16[3,128,256]{2,1,0:T(8,128)(2,1)S(1)}, bf16[3,128,256]{2,1,0:T(8,128)(2,1)S(1)}, u32[]{:S(2)}, u32[]{:S(2)}) collective-permute-start(bf16[3,128,256]{2,1,0:T(8,128)(2,1)S(1)} %get-tuple-element.110), channel_id=1, source_target_pairs={{0,4},{4,0},{8,12},{12,8},{1,5},{5,1},{9,13},{13,9},{2,6},{6,2},{1... | collective-permute-start | bytes 589832 | tf_op jit(solution)/shard_map/proj2_core1/ppermute | solution.py:103
  25.4 3.4 %collective-permute-start.15 = (bf16[2,128,256]{2,1,0:T(8,128)(2,1)S(1)}, bf16[2,128,256]{2,1,0:T(8,128)(2,1)S(1)}, u32[]{:S(2)}, u32[]{:S(2)}) collective-permute-start(bf16[2,128,256]{2,1,0:T(8,128)(2,1)S(1)} %get-tuple-element.125), channel_id=1, source_target_pairs={{0,4},{4,0},{8,12},{12,8},{1,5},{5,1},{9,13},{13,9},{2,6},{6,2},{1... | collective-permute-start | bytes 393224 | tf_op jit(solution)/shard_map/up_core/ppermute | solution.py:103
  25.7 10.6 %collective-permute-start.10 = (bf16[3,128,256]{2,1,0:T(8,128)(2,1)S(1)}, bf16[3,128,256]{2,1,0:T(8,128)(2,1)S(1)}, u32[]{:S(2)}, u32[]{:S(2)}) collective-permute-start(bf16[3,128,256]{2,1,0:T(8,128)(2,1)S(1)} %get-tuple-element.112), channel_id=1, source_target_pairs={{0,8},{4,12},{8,0},{12,4},{1,9},{5,13},{9,1},{13,5},{2,10},{6,14},... | collective-permute-start | bytes 589832 | tf_op jit(solution)/shard_map/proj2_y/ppermute | solution.py:103
  28.3 2.0 %collective-permute-start.12 = (bf16[3,128,256]{2,1,0:T(8,128)(2,1)S(1)}, bf16[3,128,256]{2,1,0:T(8,128)(2,1)S(1)}, u32[]{:S(2)}, u32[]{:S(2)}) collective-permute-start(bf16[3,128,256]{2,1,0:T(8,128)(2,1)S(1)} %get-tuple-element.119), channel_id=1, source_target_pairs={{0,4},{4,0},{8,12},{12,8},{1,5},{5,1},{9,13},{13,9},{2,6},{6,2},{1... | collective-permute-start | bytes 589832 | tf_op jit(solution)/shard_map/proj3_core0/ppermute | solution.py:103
  28.4 3.3 %collective-permute-start.13 = (bf16[3,128,256]{2,1,0:T(8,128)(2,1)S(1)}, bf16[3,128,256]{2,1,0:T(8,128)(2,1)S(1)}, u32[]{:S(2)}, u32[]{:S(2)}) collective-permute-start(bf16[3,128,256]{2,1,0:T(8,128)(2,1)S(1)} %get-tuple-element.121), channel_id=1, source_target_pairs={{0,4},{4,0},{8,12},{12,8},{1,5},{5,1},{9,13},{13,9},{2,6},{6,2},{1... | collective-permute-start | bytes 589832 | tf_op jit(solution)/shard_map/proj3_core1/ppermute | solution.py:103
  28.9 7.4 %collective-permute-start.16 = (bf16[2,128,256]{2,1,0:T(8,128)(2,1)S(1)}, bf16[2,128,256]{2,1,0:T(8,128)(2,1)S(1)}, u32[]{:S(2)}, u32[]{:S(2)}) collective-permute-start(bf16[2,128,256]{2,1,0:T(8,128)(2,1)S(1)} %pad_maximum_fusion), channel_id=1, source_target_pairs={{0,8},{4,12},{8,0},{12,4},{1,9},{5,13},{9,1},{13,5},{2,10},{6,14},... | collective-permute-start | bytes 393224 | tf_op jit(solution)/shard_map/up_y/ppermute | solution.py:103
  29.6 10.6 %copy-start = (f32[3,3,1024]{2,1,0:T(4,128)S(1)}, f32[3,3,1024]{2,1,0:T(4,128)}, u32[]{:S(2)}) copy-start(f32[3,3,1024]{2,1,0:T(4,128)} %refs_3_.3) | copy-start | bytes 110596
  29.6 10.6 %copy-start.1 = (f32[7,1024]{1,0:T(8,128)S(1)}, f32[7,1024]{1,0:T(8,128)}, u32[]{:S(2)}) copy-start(f32[7,1024]{1,0:T(8,128)} %refs_4_.3) | copy-start | bytes 86020
  30.3 9.9 %collective-permute-start.18 = (bf16[1024,128]{1,0:T(8,128)(2,1)S(1)}, bf16[1024,128]{1,0:T(8,128)(2,1)S(1)}, u32[]{:S(2)}, u32[]{:S(2)}) collective-permute-start(bf16[1024,128]{1,0:T(8,128)(2,1)S(1)} %get-tuple-element.133.refs_2_), channel_id=1, source_target_pairs={{0,16},{16,0},{1,17},{17,1},{2,18},{18,2},{3,19},{19,3},{4,20},{20... | collective-permute-start | bytes 786440 | tf_op jit(solution)/shard_map/proj2_xt_x/ppermute | solution.py:103
  31.7 8.1 %collective-permute-start.14 = (bf16[3,128,256]{2,1,0:T(8,128)(2,1)S(1)}, bf16[3,128,256]{2,1,0:T(8,128)(2,1)S(1)}, u32[]{:S(2)}, u32[]{:S(2)}) collective-permute-start(bf16[3,128,256]{2,1,0:T(8,128)(2,1)S(1)} %get-tuple-element.123), channel_id=1, source_target_pairs={{0,8},{4,12},{8,0},{12,4},{1,9},{5,13},{9,1},{13,5},{2,10},{6,14},... | collective-permute-start | bytes 589832 | tf_op jit(solution)/shard_map/proj3_y/ppermute | solution.py:103
  36.4 8.8 %collective-permute-start.23 = (bf16[1024,128]{1,0:T(8,128)(2,1)S(1)}, bf16[1024,128]{1,0:T(8,128)(2,1)S(1)}, u32[]{:S(2)}, u32[]{:S(2)}) collective-permute-start(bf16[1024,128]{1,0:T(8,128)(2,1)S(1)} %get-tuple-element.140.refs_3_), channel_id=1, source_target_pairs={{0,16},{16,0},{1,17},{17,1},{2,18},{18,2},{3,19},{19,3},{4,20},{20... | collective-permute-start | bytes 786440 | tf_op jit(solution)/shard_map/proj3_xt_x/ppermute | solution.py:103
  40.8 6.3 %collective-permute-start.21 = (bf16[3,128,256]{2,1,0:T(8,128)(2,1)S(1)}, bf16[3,128,256]{2,1,0:T(8,128)(2,1)S(1)}, u32[]{:S(2)}, u32[]{:S(2)}) collective-permute-start(bf16[3,128,256]{2,1,0:T(8,128)(2,1)S(1)} %get-tuple-element.134.refs_5_), channel_id=1, source_target_pairs={{0,8},{4,12},{8,0},{12,4},{1,9},{5,13},{9,1},{13,5},{2,10},{6,14},... | collective-permute-start | bytes 589832 | tf_op jit(solution)/shard_map/g1_y/ppermute | solution.py:103
  43.2 10.0 %collective-permute-start.19 = (bf16[2,3,128,256]{3,2,1,0:T(8,128)(2,1)S(1)}, bf16[2,3,128,256]{3,2,1,0:T(8,128)(2,1)S(1)}, u32[]{:S(2)}, u32[]{:S(2)}) collective-permute-start(bf16[2,3,128,256]{3,2,1,0:T(8,128)(2,1)S(1)} %get-tuple-element.137.refs_0_), channel_id=1, source_target_pairs={{0,4},{4,0},{8,12},{12,8},{1,5},{5,1},{9,13},{13,9},{2,6},{6,2},{1... | collective-permute-start | bytes 1179656 | tf_op jit(solution)/shard_map/g30_core/ppermute | solution.py:103
  43.3 3.9 %collective-permute-start.26 = (bf16[3,128,256]{2,1,0:T(8,128)(2,1)S(1)}, bf16[3,128,256]{2,1,0:T(8,128)(2,1)S(1)}, u32[]{:S(2)}, u32[]{:S(2)}) collective-permute-start(bf16[3,128,256]{2,1,0:T(8,128)(2,1)S(1)} %get-tuple-element.138.refs_0_), channel_id=1, source_target_pairs={{0,4},{4,0},{8,12},{12,8},{1,5},{5,1},{9,13},{13,9},{2,6},{6,2},{1... | collective-permute-start | bytes 589832 | tf_op jit(solution)/shard_map/g2_core/ppermute | solution.py:103
  43.7 19.5 %collective-permute-start.25 = (bf16[4,3,128,256]{3,2,1,0:T(8,128)(2,1)S(1)}, bf16[4,3,128,256]{3,2,1,0:T(8,128)(2,1)S(1)}, u32[]{:S(2)}, u32[]{:S(2)}) collective-permute-start(bf16[4,3,128,256]{3,2,1,0:T(8,128)(2,1)S(1)} %get-tuple-element.136.refs_1_.refs_4_), channel_id=1, source_target_pairs={{0,16},{16,0},{1,17},{17,1},{2,18},{18,2},{3,19},{19,3},{4,20},{20... | collective-permute-start | bytes 2359304 | tf_op jit(solution)/shard_map/g_x/ppermute | solution.py:103
  45.2 2.6 %collective-permute-start.20 = (bf16[3,128,256]{2,1,0:T(8,128)(2,1)S(1)}, bf16[3,128,256]{2,1,0:T(8,128)(2,1)S(1)}, u32[]{:S(2)}, u32[]{:S(2)}) collective-permute-start(bf16[3,128,256]{2,1,0:T(8,128)(2,1)S(1)} %get-tuple-element.134.refs_5_), channel_id=1, source_target_pairs={{0,4},{4,0},{8,12},{12,8},{1,5},{5,1},{9,13},{13,9},{2,6},{6,2},{1... | collective-permute-start | bytes 589832 | tf_op jit(solution)/shard_map/g1_core/ppermute | solution.py:103
  47.1 1.4 %collective-permute-start.22 = (bf16[3,128,256]{2,1,0:T(8,128)(2,1)S(1)}, bf16[3,128,256]{2,1,0:T(8,128)(2,1)S(1)}, u32[]{:S(2)}, u32[]{:S(2)}) collective-permute-start(bf16[3,128,256]{2,1,0:T(8,128)(2,1)S(1)} %collective-permute-done.21.refs_2_.refs_3_.refs_8_), channel_id=1, source_target_pairs={{0,4},{4,0},{8,12},{12,8},{1,5},{5,1},{9,13},{13,9},{2,6},{6,2},{1... | collective-permute-start | bytes 589832 | tf_op jit(solution)/shard_map/gy1_core/ppermute | solution.py:103
  47.1 7.3 %collective-permute-start.27 = (bf16[3,128,256]{2,1,0:T(8,128)(2,1)S(1)}, bf16[3,128,256]{2,1,0:T(8,128)(2,1)S(1)}, u32[]{:S(2)}, u32[]{:S(2)}) collective-permute-start(bf16[3,128,256]{2,1,0:T(8,128)(2,1)S(1)} %get-tuple-element.144), channel_id=1, source_target_pairs={{0,8},{4,12},{8,0},{12,4},{1,9},{5,13},{9,1},{13,5},{2,10},{6,14},... | collective-permute-start | bytes 589832 | tf_op jit(solution)/shard_map/g2_y/ppermute | solution.py:103
  50.8 8.6 %collective-permute-start.29 = (bf16[128,1024]{1,0:T(8,128)(2,1)S(1)}, bf16[128,1024]{1,0:T(8,128)(2,1)S(1)}, u32[]{:S(2)}, u32[]{:S(2)}) collective-permute-start(bf16[128,1024]{1,0:T(8,128)(2,1)S(1)} %get-tuple-element.148), channel_id=1, source_target_pairs={{0,2},{2,3},{3,1},{1,0},{4,6},{6,7},{7,5},{5,4},{8,10},{10,11},{11... | collective-permute-start | bytes 786440 | tf_op jit(solution)/shard_map/share1/ppermute | solution.py:112
  53.2 10.9 %collective-permute-start.24 = (bf16[2,3,128,256]{3,2,1,0:T(8,128)(2,1)S(1)}, bf16[2,3,128,256]{3,2,1,0:T(8,128)(2,1)S(1)}, u32[]{:S(2)}, u32[]{:S(2)}) collective-permute-start(bf16[2,3,128,256]{3,2,1,0:T(8,128)(2,1)S(1)} %get-tuple-element.143), channel_id=1, source_target_pairs={{0,8},{4,12},{8,0},{12,4},{1,9},{5,13},{9,1},{13,5},{2,10},{6,14},... | collective-permute-start | bytes 1179656 | tf_op jit(solution)/shard_map/g30_y/ppermute | solution.py:103
  54.5 2.0 %collective-permute-start.28 = (bf16[3,128,256]{2,1,0:T(8,128)(2,1)S(1)}, bf16[3,128,256]{2,1,0:T(8,128)(2,1)S(1)}, u32[]{:S(2)}, u32[]{:S(2)}) collective-permute-start(bf16[3,128,256]{2,1,0:T(8,128)(2,1)S(1)} %collective-permute-done.27.refs_3_.refs_9_), channel_id=1, source_target_pairs={{0,4},{4,0},{8,12},{12,8},{1,5},{5,1},{9,13},{13,9},{2,6},{6,2},{1... | collective-permute-start | bytes 589832 | tf_op jit(solution)/shard_map/gy2_core/ppermute | solution.py:103
  64.1 4.7 %collective-permute-start.30 = (bf16[2,3,128,256]{3,2,1,0:T(8,128)(2,1)S(1)}, bf16[2,3,128,256]{3,2,1,0:T(8,128)(2,1)S(1)}, u32[]{:S(2)}, u32[]{:S(2)}) collective-permute-start(bf16[2,3,128,256]{3,2,1,0:T(8,128)(2,1)S(1)} %get-tuple-element.152.refs_3_.refs_7_), channel_id=1, source_target_pairs={{0,4},{4,0},{8,12},{12,8},{1,5},{5,1},{9,13},{13,9},{2,6},{6,2},{1... | collective-permute-start | bytes 1179656 | tf_op jit(solution)/shard_map/gy30_core/ppermute | solution.py:103
  64.1 6.7 %collective-permute-start.32 = (bf16[4,3,128,256]{3,2,1,0:T(8,128)(2,1)S(1)}, bf16[4,3,128,256]{3,2,1,0:T(8,128)(2,1)S(1)}, u32[]{:S(2)}, u32[]{:S(2)}) collective-permute-start(bf16[4,3,128,256]{3,2,1,0:T(8,128)(2,1)S(1)} %get-tuple-element.157.refs_4_), channel_id=1, source_target_pairs={{0,4},{4,0},{8,12},{12,8},{1,5},{5,1},{9,13},{13,9},{2,6},{6,2},{1... | collective-permute-start | bytes 2359304 | tf_op jit(solution)/shard_map/gx_core/ppermute | solution.py:103
  64.6 10.7 %collective-permute-start.31 = (bf16[128,1024]{1,0:T(8,128)(2,1)S(1)}, bf16[128,1024]{1,0:T(8,128)(2,1)S(1)}, u32[]{:S(2)}, u32[]{:S(2)}) collective-permute-start(bf16[128,1024]{1,0:T(8,128)(2,1)S(1)} %get-tuple-element.156), channel_id=1, source_target_pairs={{0,2},{2,3},{3,1},{1,0},{4,6},{6,7},{7,5},{5,4},{8,10},{10,11},{11... | collective-permute-start | bytes 786440 | tf_op jit(solution)/shard_map/share2/ppermute | solution.py:112
  67.1 12.1 %collective-permute-start.35 = (bf16[2,3,128,256]{3,2,1,0:T(8,128)(2,1)S(1)}, bf16[2,3,128,256]{3,2,1,0:T(8,128)(2,1)S(1)}, u32[]{:S(2)}, u32[]{:S(2)}) collective-permute-start(bf16[2,3,128,256]{3,2,1,0:T(8,128)(2,1)S(1)} %get-tuple-element.152.refs_3_.refs_7_), channel_id=1, source_target_pairs={{0,16},{16,0},{1,17},{17,1},{2,18},{18,2},{3,19},{19,3},{4,20},{20... | collective-permute-start | bytes 1179656 | tf_op jit(solution)/shard_map/gy30_x/ppermute | solution.py:103
  68.6 10.5 %collective-permute-start.34 = (bf16[2,3,128,256]{3,2,1,0:T(8,128)(2,1)S(1)}, bf16[2,3,128,256]{3,2,1,0:T(8,128)(2,1)S(1)}, u32[]{:S(2)}, u32[]{:S(2)}) collective-permute-start(bf16[2,3,128,256]{3,2,1,0:T(8,128)(2,1)S(1)} %slice.19), channel_id=1, source_target_pairs={{0,8},{4,12},{8,0},{12,4},{1,9},{5,13},{9,1},{13,5},{2,10},{6,14},... | collective-permute-start | bytes 1179656 | tf_op jit(solution)/shard_map/gx12_y/ppermute | solution.py:103
  79.2 1.7 %collective-permute-start.36 = (bf16[2,3,128,256]{3,2,1,0:T(8,128)(2,1)S(1)}, bf16[2,3,128,256]{3,2,1,0:T(8,128)(2,1)S(1)}, u32[]{:S(2)}, u32[]{:S(2)}) collective-permute-start(bf16[2,3,128,256]{3,2,1,0:T(8,128)(2,1)S(1)} %get-tuple-element.163.refs_10_), channel_id=1, source_target_pairs={{0,4},{4,0},{8,12},{12,8},{1,5},{5,1},{9,13},{13,9},{2,6},{6,2},{1... | collective-permute-start | bytes 1179656 | tf_op jit(solution)/shard_map/gxy30_core/ppermute | solution.py:103
  79.2 2.3 %collective-permute-start.37 = (bf16[2,3,128,256]{3,2,1,0:T(8,128)(2,1)S(1)}, bf16[2,3,128,256]{3,2,1,0:T(8,128)(2,1)S(1)}, u32[]{:S(2)}, u32[]{:S(2)}) collective-permute-start(bf16[2,3,128,256]{3,2,1,0:T(8,128)(2,1)S(1)} %get-tuple-element.164.refs_11_), channel_id=1, source_target_pairs={{0,4},{4,0},{8,12},{12,8},{1,5},{5,1},{9,13},{13,9},{2,6},{6,2},{1... | collective-permute-start | bytes 1179656 | tf_op jit(solution)/shard_map/gxy12_core/ppermute | solution.py:103
  79.7 8.3 %collective-permute-start.33 = (bf16[128,1024]{1,0:T(8,128)(2,1)S(1)}, bf16[128,1024]{1,0:T(8,128)(2,1)S(1)}, u32[]{:S(2)}, u32[]{:S(2)}) collective-permute-start(bf16[128,1024]{1,0:T(8,128)(2,1)S(1)} %get-tuple-element.161), channel_id=1, source_target_pairs={{0,2},{2,3},{3,1},{1,0},{4,6},{6,7},{7,5},{5,4},{8,10},{10,11},{11... | collective-permute-start | bytes 786440 | tf_op jit(solution)/shard_map/share3/ppermute | solution.py:112
where the time goes:
time: 88.9 us; the launch traced here: 88.7 us
  starting transfers between devices  34 us (38%)
  Pallas kernels  31.3 us (35%)
  waiting for transfers between devices  22.3 us (25%)
  between operations  0.97 us (1%)
    pallas_call x33, Pallas kernels, local(): pl.pallas_call(ordered, out_shape=[jax.ShapeDtypeStruct((8, LANES), jnp.f...  31.3 us
    ppermute x32, starting transfers between devices, swap(): return lax.ppermute(value, axis, [(i, i ^ step) for i in range(size)])  20.6 us
    ppermute x32, waiting for transfers between devices, swap(): return lax.ppermute(value, axis, [(i, i ^ step) for i in range(size)])  19.2 us
    ppermute x6, starting transfers between devices, along(): return lax.ppermute(value, 'col', pairs)  13.4 us
    ppermute x6, waiting for transfers between devices, along(): return lax.ppermute(value, 'col', pairs)  3.12 us
  transfers between devices with their start and end apart: 38, of which 20 were waited for; matrix products, arithmetic and copies ran while one was open for 0% of the time, Pallas kernels for 34%

commit v1 on v0

--- a/solution.py
+++ b/solution.py
@@ -376,7 +376,7 @@
         body,
         [bf16(high, depth)] * shards,
         [*(g for g, _ in pieces), w],
-        6.0 if shards > 1 else 0.8,
+        0.3 if shards > 1 else 0.8,
         scratch=[pltpu.VMEM((parts, shards * high, width), jnp.bfloat16)],
         late=late,
     )
@@ -470,12 +470,22 @@
         body,
         [out],
         ins,
-        6.0 if final else 4.0,
+        (6.0 if done is not None else 0.3) if final else 4.0,
         specs,
         scratch=scratch,
         out_specs=[ANY if final else VMEM],
         aliases=aliases,
     )
+    return me, out
+
+
+def first_half(me, value):
+    shape = (value.shape[0] // 2, *value.shape[1:])
+
+    def body(value_ref, out_ref):
+        out_ref[...] = value_ref[: shape[0]]
+
+    me, (out,) = local(me, body, [bf16(*shape)], [value], 0.05, placed=False)
     return me, out
 
 
@@ -581,7 +591,9 @@
     passed = send("share2", share2, "col", 1)
     with jax.named_scope("relay_x"):
         me, (x,) = relay(me, x)
-    xy12, cx = send("gx12_y", x[:2], "row", CORES), send("gx_core", x, "row", 1)
+    with jax.named_scope("first_half"):
+        me, x12 = first_half(me, x)
+    xy12, cx = send("gx12_y", x12, "row", CORES), send("gx_core", x, "row", 1)
     with jax.named_scope("relay_y30"):
         me, (y30,) = relay(me, y30)
     xy30, cy30 = send("gy30_x", y30, "dp", 1), send("gy30_core", y30, "row", 1)
@@ -592,7 +604,7 @@
         blocks = [(0, whole(x)), (1, whole(cx))]
         me, grad_w = weight_grads(me, None, others, blocks, width, begun)
     with jax.named_scope("total3"):
-        me, share3 = total(me, [share3, passed])
+        me, share3 = total(me, [share3, passed], [xy12])
     passed = send("share3", share3, "col", 1)
     with jax.named_scope("relay_xy"):
         me, (xy12, xy30) = relay(me, xy12, xy30)

time: 88.9 us -> 86.1 us (0.969)
  waiting for transfers between devices: 22.3 us -> 17.9 us
  starting transfers between devices: 34 us -> 35.6 us
    ppermute x32, waiting for transfers between devices: 19.2 us -> 15 us  [swap(): return lax.ppermute(value, axis, [(i, i ^ step) for i in range(size)])]
    ppermute x6, starting transfers between devices: 13.4 us -> 14.6 us  [along(): return lax.ppermute(value, 'col', pairs)]
    pallas_call x33 -> x34, Pallas kernels: 31.3 us -> 31.4 us  [local(): pl.pallas_call(ordered, out_shape=[jax.ShapeDtypeStruct((8, LANES), jnp.f...]
  transfers between devices with their start and end apart: 38 -> 38, of which waited for: 20 -> 19; matrix products, arithmetic and copies ran while one was open for 0% -> 0% of each run, Pallas kernels for 34% -> 36%
where the time goes in v1:
time: 86.1 us; the launch traced here: 86 us
  starting transfers between devices  35.6 us (41%)
  Pallas kernels  31.4 us (36%)
  waiting for transfers between devices  17.9 us (21%)
  between operations  0.97 us (1%)
    pallas_call x34, Pallas kernels, local(): pl.pallas_call(ordered, out_shape=[jax.ShapeDtypeStruct((8, LANES), jnp.f...  31.4 us
    ppermute x32, starting transfers between devices, swap(): return lax.ppermute(value, axis, [(i, i ^ step) for i in range(size)])  21 us
    ppermute x32, waiting for transfers between devices, swap(): return lax.ppermute(value, axis, [(i, i ^ step) for i in range(size)])  15 us
    ppermute x6, starting transfers between devices, along(): return lax.ppermute(value, 'col', pairs)  14.6 us
    ppermute x6, waiting for transfers between devices, along(): return lax.ppermute(value, 'col', pairs)  2.86 us
  transfers between devices with their start and end apart: 38, of which 19 were waited for; matrix products, arithmetic and copies ran while one was open for 0% of the time, Pallas kernels for 36%

profile of v1, /device:TPU:0, one launch (start us, length us, event | category | flops | bytes accessed | tf_op | source)
XLA Modules:
  0.0 86.0 jit_solution(10082346953316194154)
XLA Ops:
  0.6 4.1 %collective-permute-start.3 = (bf16[128,1024]{1,0:T(8,128)(2,1)}, bf16[128,1024]{1,0:T(8,128)(2,1)S(1)}, u32[]{:S(2)}, u32[]{:S(2)}) collective-permute-start(bf16[128,1024]{1,0:T(8,128)(2,1)} %bitcast.18), channel_id=1, source_target_pairs={{0,2},{2,3},{3,1},{1,0},{4,6},{6,7},{7,5},{5,4},{8,10},{10,11},{11... | collective-permute-start | bytes 786440 | tf_op jit(solution)/shard_map/x1/ppermute | solution.py:112
  4.8 4.0 %begin.1 = (f32[8,128]{1,0:T(8,128)S(1)}, bf16[3,1024,1024]{2,1,0:T(8,128)(2,1)S(1)}, bf16[128,1024]{1,0:T(8,128)(2,1)S(1)}, bf16[2,128,256]{2,1,0:T(8,128)(2,1)...) custom-call(s32[2]{0:T(128)S(1)} %pad_add_fusion.refs_0_, ...), custom_call_target="tpu_custom_call" | custom-call | flops 3849999872 | bytes 1 | tf_op jit(solution)/shard_map/begin/pallas_call | solution.py:151
  8.8 0.5 collective-permute-start.1
  9.3 0.6 proj0_keep.1
  10.0 0.3 collective-permute-done.refs_3_.refs_2_
  10.3 0.3 collective-permute-done.1.refs_1_
  10.6 1.6 %collective-permute-start.2 = (bf16[3,128,256]{2,1,0:T(8,128)(2,1)S(1)}, bf16[3,128,256]{2,1,0:T(8,128)(2,1)S(1)}, u32[]{:S(2)}, u32[]{:S(2)}) collective-permute-start(bf16[3,128,256]{2,1,0:T(8,128)(2,1)S(1)} %get-tuple-element.97), channel_id=1, source_target_pairs={{0,8},{4,12},{8,0},{12,4},{1,9},{5,13},{9,1},{13,5},{2,10},{6,14},... | collective-permute-start | bytes 589832 | tf_op jit(solution)/shard_map/proj0_y/ppermute | solution.py:103
  12.2 1.7 %collective-permute-start.7 = (bf16[128,1024]{1,0:T(8,128)(2,1)S(1)}, bf16[128,1024]{1,0:T(8,128)(2,1)S(1)}, u32[]{:S(2)}, u32[]{:S(2)}) collective-permute-start(bf16[128,1024]{1,0:T(8,128)(2,1)S(1)} %collective-permute-done.3.refs_1_), channel_id=1, source_target_pairs={{0,2},{2,3},{3,1},{1,0},{4,6},{6,7},{7,5},{5,4},{8,10},{10,11},{11... | collective-permute-start | bytes 786440 | tf_op jit(solution)/shard_map/x2/ppermute | solution.py:112
  13.9 0.6 proj1_away.1
  14.6 0.5 collective-permute-start.5
  15.1 0.6 proj1_keep.1
  15.7 0.3 collective-permute-done.4.refs_3_.refs_5_
  16.0 0.3 collective-permute-done.5.refs_1_
  16.3 1.6 %collective-permute-start.6 = (bf16[3,128,256]{2,1,0:T(8,128)(2,1)S(1)}, bf16[3,128,256]{2,1,0:T(8,128)(2,1)S(1)}, u32[]{:S(2)}, u32[]{:S(2)}) collective-permute-start(bf16[3,128,256]{2,1,0:T(8,128)(2,1)S(1)} %get-tuple-element.105), channel_id=1, source_target_pairs={{0,8},{4,12},{8,0},{12,4},{1,9},{5,13},{9,1},{13,5},{2,10},{6,14},... | collective-permute-start | bytes 589832 | tf_op jit(solution)/shard_map/proj1_y/ppermute | solution.py:103
  17.9 0.2 proj1_turned.1
  18.1 1.6 %collective-permute-start.17 = (bf16[1024,256]{1,0:T(8,128)(2,1)S(1)}, bf16[1024,256]{1,0:T(8,128)(2,1)S(1)}, u32[]{:S(2)}, u32[]{:S(2)}) collective-permute-start(bf16[1024,256]{1,0:T(8,128)(2,1)S(1)} %get-tuple-element.130.refs_1_), channel_id=1, source_target_pairs={{0,16},{16,0},{1,17},{17,1},{2,18},{18,2},{3,19},{19,3},{4,20},{20... | collective-permute-start | bytes 1572872 | tf_op jit(solution)/shard_map/proj1_xt_x/ppermute | solution.py:103
  19.7 0.7 collective-permute-done.7.refs_1_.refs_0_
  20.4 2.5 %collective-permute-start.11 = (bf16[128,1024]{1,0:T(8,128)(2,1)S(1)}, bf16[128,1024]{1,0:T(8,128)(2,1)S(1)}, u32[]{:S(2)}, u32[]{:S(2)}) collective-permute-start(bf16[128,1024]{1,0:T(8,128)(2,1)S(1)} %collective-permute-done.7.refs_1_.refs_0_), channel_id=1, source_target_pairs={{0,2},{2,3},{3,1},{1,0},{4,6},{6,7},{7,5},{5,4},{8,10},{10,11},{11... | collective-permute-start | bytes 786440 | tf_op jit(solution)/shard_map/x3/ppermute | solution.py:112
  22.8 0.6 proj2_away.1
  23.5 0.5 collective-permute-start.9
  24.0 0.6 proj2_keep.1
  24.6 0.3 collective-permute-done.8.refs_3_.refs_8_
  24.9 0.3 collective-permute-done.9.refs_1_
  25.4 0.3 collective-permute-start.15
  25.7 0.7 collective-permute-start.10
  26.4 1.3 %collective-permute-done.11.refs_1_.refs_0_ = bf16[128,1024]{1,0:T(8,128)(2,1)S(1)} collective-permute-done((bf16[128,1024]{1,0:T(8,128)(2,1)S(1)}, bf16[128,1024]{1,0:T(8,128)(2,1)S(1)}, u32[]{:S(2)}, u32[]{:S(2)}) %collective-permute-start.11) | collective-permute-done | bytes 262176 | tf_op jit(solution)/shard_map/x3/ppermute | solution.py:112
  27.7 0.6 proj3_away.1
  28.4 0.5 collective-permute-start.13
  28.9 0.7 collective-permute-start.16
  29.6 0.6 proj3_keep.1
  30.3 1.4 %collective-permute-start.18 = (bf16[1024,128]{1,0:T(8,128)(2,1)S(1)}, bf16[1024,128]{1,0:T(8,128)(2,1)S(1)}, u32[]{:S(2)}, u32[]{:S(2)}) collective-permute-start(bf16[1024,128]{1,0:T(8,128)(2,1)S(1)} %get-tuple-element.135.refs_2_), channel_id=1, source_target_pairs={{0,16},{16,0},{1,17},{17,1},{2,18},{18,2},{3,19},{19,3},{4,20},{20... | collective-permute-start | bytes 786440 | tf_op jit(solution)/shard_map/proj2_xt_x/ppermute | solution.py:103
  31.7 1.6 %collective-permute-start.14 = (bf16[3,128,256]{2,1,0:T(8,128)(2,1)S(1)}, bf16[3,128,256]{2,1,0:T(8,128)(2,1)S(1)}, u32[]{:S(2)}, u32[]{:S(2)}) collective-permute-start(bf16[3,128,256]{2,1,0:T(8,128)(2,1)S(1)} %get-tuple-element.125), channel_id=1, source_target_pairs={{0,8},{4,12},{8,0},{12,4},{1,9},{5,13},{9,1},{13,5},{2,10},{6,14},... | collective-permute-start | bytes 589832 | tf_op jit(solution)/shard_map/proj3_y/ppermute | solution.py:103
  33.3 3.0 %collective-permute-done.16 = bf16[2,128,256]{2,1,0:T(8,128)(2,1)S(1)} collective-permute-done((bf16[2,128,256]{2,1,0:T(8,128)(2,1)S(1)}, bf16[2,128,256]{2,1,0:T(8,128)(2,1)S(1)}, u32[]{:S(2)}, u32[]{:S(2)}) %collective-permute-start.16) | collective-permute-done | bytes 131104 | tf_op jit(solution)/shard_map/up_y/ppermute | solution.py:103
  36.4 1.6 %collective-permute-start.23 = (bf16[1024,128]{1,0:T(8,128)(2,1)S(1)}, bf16[1024,128]{1,0:T(8,128)(2,1)S(1)}, u32[]{:S(2)}, u32[]{:S(2)}) collective-permute-start(bf16[1024,128]{1,0:T(8,128)(2,1)S(1)} %get-tuple-element.142.refs_3_), channel_id=1, source_target_pairs={{0,16},{16,0},{1,17},{17,1},{2,18},{18,2},{3,19},{19,3},{4,20},{20... | collective-permute-start | bytes 786440 | tf_op jit(solution)/shard_map/proj3_xt_x/ppermute | solution.py:103
  38.0 1.9 %collective-permute-done.14.refs_12_ = bf16[3,128,256]{2,1,0:T(8,128)(2,1)S(1)} collective-permute-done((bf16[3,128,256]{2,1,0:T(8,128)(2,1)S(1)}, bf16[3,128,256]{2,1,0:T(8,128)(2,1)S(1)}, u32[]{:S(2)}, u32[]{:S(2)}) %collective-permute-start.14) | collective-permute-done | bytes 196640 | tf_op jit(solution)/shard_map/proj3_y/ppermute | solution.py:103
  39.8 0.4 laid_out.1
  40.2 0.6 gate1.1
  40.8 0.7 collective-permute-start.21
  41.5 1.7 %gate230.1 = (f32[8,128]{1,0:T(8,128)S(1)}, bf16[4,3,128,256]{3,2,1,0:T(8,128)(2,1)S(1)}, bf16[2,3,128,256]{3,2,1,0:T(8,128)(2,1)S(1)}, bf16[3,128,256]{2,1,0:T(8,128)(2,1)S(1)}) custom-call(s32[2]{0:T(128)S(4)} %get-tuple-element.88.refs_0_, f32[3,528,256]{2,1,0:T(8,128)S(1)} %get-tuple-element.132.refs_1_, ...), custom_call_target="tpu_custom_call", output_to_operand_aliasing={{0}: (6, {})} | custom-call | flops 2640000000 | bytes 1 | tf_op jit(solution)/shard_map/gate230/pallas_call | solution.py:151
  43.3 0.5 collective-permute-start.26
  43.8 1.5 %collective-permute-start.25 = (bf16[4,3,128,256]{3,2,1,0:T(8,128)(2,1)S(1)}, bf16[4,3,128,256]{3,2,1,0:T(8,128)(2,1)S(1)}, u32[]{:S(2)}, u32[]{:S(2)}) collective-permute-start(bf16[4,3,128,256]{3,2,1,0:T(8,128)(2,1)S(1)} %get-tuple-element.138.refs_1_.refs_4_), channel_id=1, source_target_pairs={{0,16},{16,0},{1,17},{17,1},{2,18},{18,2},{3,19},{19,3},{4,20},{20... | collective-permute-start | bytes 2359304 | tf_op jit(solution)/shard_map/g_x/ppermute | solution.py:103
  45.3 1.9 %collective-permute-done.21.refs_2_.refs_3_.refs_8_ = bf16[3,128,256]{2,1,0:T(8,128)(2,1)S(1)} collective-permute-done((bf16[3,128,256]{2,1,0:T(8,128)(2,1)S(1)}, bf16[3,128,256]{2,1,0:T(8,128)(2,1)S(1)}, u32[]{:S(2)}, u32[]{:S(2)}) %collective-permute-start.21) | collective-permute-done | bytes 196640 | tf_op jit(solution)/shard_map/g1_y/ppermute | solution.py:103
  47.1 0.7 collective-permute-start.27
  47.9 0.7 collective-permute-done.22.refs_4_.refs_13_
  48.6 2.2 %input_grads1.1 = (f32[8,128]{1,0:T(8,128)S(1)}, bf16[128,1024]{1,0:T(8,128)(2,1)S(1)}) custom-call(s32[2]{0:T(128)S(4)} %get-tuple-element.88.refs_0_, bf16[4,3,128,256]{3,2,1,0:T(8,128)(2,1)S(1)} %get-tuple-element.138.refs_1_.refs_4_, bf16[3,128,256]{2,1,0:T(8,128)(2,1)S(1)} %collective-permute-done.20.refs_2_.refs_6_, ...), custom_call_target="tpu_custom_call", output_to_operand_aliasing={{0}: (6, {})} | custom-call | flops 880000000 | bytes 1 | tf_op jit(solution)/shard_map/input_grads1/pallas_call | solution.py:151
  50.8 2.4 %collective-permute-start.29 = (bf16[128,1024]{1,0:T(8,128)(2,1)S(1)}, bf16[128,1024]{1,0:T(8,128)(2,1)S(1)}, u32[]{:S(2)}, u32[]{:S(2)}) collective-permute-start(bf16[128,1024]{1,0:T(8,128)(2,1)S(1)} %get-tuple-element.150), channel_id=1, source_target_pairs={{0,2},{2,3},{3,1},{1,0},{4,6},{6,7},{7,5},{5,4},{8,10},{10,11},{11... | collective-permute-start | bytes 786440 | tf_op jit(solution)/shard_map/share1/ppermute | solution.py:112
  53.2 1.1 %collective-permute-start.24 = (bf16[2,3,128,256]{3,2,1,0:T(8,128)(2,1)S(1)}, bf16[2,3,128,256]{3,2,1,0:T(8,128)(2,1)S(1)}, u32[]{:S(2)}, u32[]{:S(2)}) collective-permute-start(bf16[2,3,128,256]{3,2,1,0:T(8,128)(2,1)S(1)} %get-tuple-element.145), channel_id=1, source_target_pairs={{0,8},{4,12},{8,0},{12,4},{1,9},{5,13},{9,1},{13,5},{2,10},{6,14},... | collective-permute-start | bytes 1179656 | tf_op jit(solution)/shard_map/g30_y/ppermute | solution.py:103
  54.5 2.0 %weight_grads_near_own.1 = (f32[8,128]{1,0:T(8,128)S(1)}, f32[3,1024,512]{2,1,0:T(8,128)S(1)}) custom-call(s32[2]{0:T(128)S(4)} %get-tuple-element.88.refs_0_, bf16[1024,256]{1,0:T(8,128)(2,1)S(1)} %get-tuple-element.130.refs_1_, bf16[1024,128]{1,0:T(8,128)(2,1)S(1)} %get-tuple-element.135.refs_2_, ...), custom_call_target="tpu_custom_call", output_to_operand_aliasing={{0}: (8, {})} | custom-call | flops 4400000000 | bytes 1 | tf_op jit(solution)/shard_map/weight_grads_near_own/pallas_call | solution.py:151
  56.5 2.2 %input_grads2.1 = (f32[8,128]{1,0:T(8,128)S(1)}, bf16[128,1024]{1,0:T(8,128)(2,1)S(1)}) custom-call(s32[2]{0:T(128)S(4)} %get-tuple-element.88.refs_0_, bf16[4,3,128,256]{3,2,1,0:T(8,128)(2,1)S(1)} %get-tuple-element.138.refs_1_.refs_4_, bf16[3,128,256]{2,1,0:T(8,128)(2,1)S(1)} %collective-permute-done.26.refs_7_.refs_2_, ...), custom_call_target="tpu_custom_call", output_to_operand_aliasing={{0}: (6, {})} | custom-call | flops 880000000 | bytes 1 | tf_op jit(solution)/shard_map/input_grads2/pallas_call | solution.py:151
  58.7 0.7 collective-permute-done.29.refs_1_
  59.5 3.8 %collective-permute-done.25.refs_0_ = bf16[4,3,128,256]{3,2,1,0:T(8,128)(2,1)S(1)} collective-permute-done((bf16[4,3,128,256]{3,2,1,0:T(8,128)(2,1)S(1)}, bf16[4,3,128,256]{3,2,1,0:T(8,128)(2,1)S(1)}, u32[]{:S(2)}, u32[]{:S(2)}) %collective-permute-start.25) | collective-permute-done | bytes 786464 | tf_op jit(solution)/shard_map/g_x/ppermute | solution.py:103
  63.3 0.8 collective-permute-done.24.refs_0_
  64.1 1.2 %collective-permute-start.33 = (bf16[2,3,128,256]{3,2,1,0:T(8,128)(2,1)S(1)}, bf16[2,3,128,256]{3,2,1,0:T(8,128)(2,1)S(1)}, u32[]{:S(2)}, u32[]{:S(2)}) collective-permute-start(bf16[2,3,128,256]{3,2,1,0:T(8,128)(2,1)S(1)} %get-tuple-element.164), channel_id=1, source_target_pairs={{0,8},{4,12},{8,0},{12,4},{1,9},{5,13},{9,1},{13,5},{2,10},{6,14},... | collective-permute-start | bytes 1179656 | tf_op jit(solution)/shard_map/gx12_y/ppermute | solution.py:103
  65.3 1.5 %collective-permute-start.35 = (bf16[2,3,128,256]{3,2,1,0:T(8,128)(2,1)S(1)}, bf16[2,3,128,256]{3,2,1,0:T(8,128)(2,1)S(1)}, u32[]{:S(2)}, u32[]{:S(2)}) collective-permute-start(bf16[2,3,128,256]{3,2,1,0:T(8,128)(2,1)S(1)} %get-tuple-element.156.refs_3_.refs_7_), channel_id=1, source_target_pairs={{0,16},{16,0},{1,17},{17,1},{2,18},{18,2},{3,19},{19,3},{4,20},{20... | collective-permute-start | bytes 1179656 | tf_op jit(solution)/shard_map/gy30_x/ppermute | solution.py:103
  66.8 2.1 %collective-permute-start.31 = (bf16[128,1024]{1,0:T(8,128)(2,1)S(1)}, bf16[128,1024]{1,0:T(8,128)(2,1)S(1)}, u32[]{:S(2)}, u32[]{:S(2)}) collective-permute-start(bf16[128,1024]{1,0:T(8,128)(2,1)S(1)} %get-tuple-element.160), channel_id=1, source_target_pairs={{0,2},{2,3},{3,1},{1,0},{4,6},{6,7},{7,5},{5,4},{8,10},{10,11},{11... | collective-permute-start | bytes 786440 | tf_op jit(solution)/shard_map/share2/ppermute | solution.py:112
  68.8 2.0 %input_grads30.1 = (f32[8,128]{1,0:T(8,128)S(1)}, bf16[128,1024]{1,0:T(8,128)(2,1)S(1)}, bf16[128,1024]{1,0:T(8,128)(2,1)S(1)}) custom-call(s32[2]{0:T(128)S(4)} %get-tuple-element.88.refs_0_, bf16[4,3,128,256]{3,2,1,0:T(8,128)(2,1)S(1)} %get-tuple-element.138.refs_1_.refs_4_, ...), custom_call_target="tpu_custom_call", output_to_operand_aliasing={{0}: (6, {})} | custom-call | flops 330000000 | bytes 1 | tf_op jit(solution)/shard_map/input_grads30/pallas_call | solution.py:151
  70.8 4.5 %weight_grads_near.1 = (f32[8,128]{1,0:T(8,128)S(1)}, f32[3,1024,1024]{2,1,0:T(8,128)}) custom-call(s32[2]{0:T(128)S(4)} %get-tuple-element.88.refs_0_, bf16[1024,256]{1,0:T(8,128)(2,1)S(1)} %collective-permute-done.17.refs_3_.refs_1_.refs_4_, bf16[1024,128]{1,0:T(8,128)(2,1)S(1)} %collective-permute-done.18.refs_6_.refs_2_.refs_5_, ...), custom_call_target="tpu_custom_call", output_to_operand_aliasing={{0}: (7, {})} | custom-call | flops 330000000 | bytes 1 | tf_op jit(solution)/shard_map/weight_grads_near/pallas_call | solution.py:151
  75.4 0.3 collective-permute-done.33.refs_3_.refs_0_
  75.7 0.8 collective-permute-done.35.refs_1_
  76.5 0.5 collective-permute-start.37
  77.0 1.9 %collective-permute-start.34 = (bf16[128,1024]{1,0:T(8,128)(2,1)S(1)}, bf16[128,1024]{1,0:T(8,128)(2,1)S(1)}, u32[]{:S(2)}, u32[]{:S(2)}) collective-permute-start(bf16[128,1024]{1,0:T(8,128)(2,1)S(1)} %get-tuple-element.165), channel_id=1, source_target_pairs={{0,2},{2,3},{3,1},{1,0},{4,6},{6,7},{7,5},{5,4},{8,10},{10,11},{11... | collective-permute-start | bytes 786440 | tf_op jit(solution)/shard_map/share3/ppermute | solution.py:112
  78.9 6.1 %weight_grads_far.1 = (f32[8,128]{1,0:T(8,128)S(1)}, f32[3,1024,1024]{2,1,0:T(8,128)}) custom-call(s32[2]{0:T(128)S(4)} %get-tuple-element.88.refs_0_, bf16[1024,256]{1,0:T(8,128)(2,1)S(1)} %get-tuple-element.130.refs_1_, bf16[1024,128]{1,0:T(8,128)(2,1)S(1)} %get-tuple-element.135.refs_2_, ...), custom_call_target="tpu_custom_call", output_to_operand_aliasing={{0}: (18, {}), {1}: (17, {})} | custom-call | flops 6600000000 | bytes 1 | tf_op jit(solution)/shard_map/weight_grads_far/pallas_call | solution.py:151
  85.0 0.2 collective-permute-done.34.refs_1_
  85.2 0.8 total0.1
  (54 shorter events, 1.2 us)
Async XLA Ops:
  0.6 11.6 %collective-permute-start.3 = (bf16[128,1024]{1,0:T(8,128)(2,1)}, bf16[128,1024]{1,0:T(8,128)(2,1)S(1)}, u32[]{:S(2)}, u32[]{:S(2)}) collective-permute-start(bf16[128,1024]{1,0:T(8,128)(2,1)} %bitcast.18), channel_id=1, source_target_pairs={{0,2},{2,3},{3,1},{1,0},{4,6},{6,7},{7,5},{5,4},{8,10},{10,11},{11... | collective-permute-start | bytes 786440 | tf_op jit(solution)/shard_map/x1/ppermute | solution.py:112
  8.8 1.5 %collective-permute-start = (bf16[3,128,256]{2,1,0:T(8,128)(2,1)S(1)}, bf16[3,128,256]{2,1,0:T(8,128)(2,1)S(1)}, u32[]{:S(2)}, u32[]{:S(2)}) collective-permute-start(bf16[3,128,256]{2,1,0:T(8,128)(2,1)S(1)} %get-tuple-element.93), channel_id=1, source_target_pairs={{0,4},{4,0},{8,12},{12,8},{1,5},{5,1},{9,13},{13,9},{2,6},{6,2},{1... | collective-permute-start | bytes 589832 | tf_op jit(solution)/shard_map/proj0_core0/ppermute | solution.py:103
  8.8 1.7 %collective-permute-start.1 = (bf16[3,128,256]{2,1,0:T(8,128)(2,1)S(1)}, bf16[3,128,256]{2,1,0:T(8,128)(2,1)S(1)}, u32[]{:S(2)}, u32[]{:S(2)}) collective-permute-start(bf16[3,128,256]{2,1,0:T(8,128)(2,1)S(1)} %get-tuple-element.95), channel_id=1, source_target_pairs={{0,4},{4,0},{8,12},{12,8},{1,5},{5,1},{9,13},{13,9},{2,6},{6,2},{1... | collective-permute-start | bytes 589832 | tf_op jit(solution)/shard_map/proj0_core1/ppermute | solution.py:103
  10.6 7.3 %collective-permute-start.2 = (bf16[3,128,256]{2,1,0:T(8,128)(2,1)S(1)}, bf16[3,128,256]{2,1,0:T(8,128)(2,1)S(1)}, u32[]{:S(2)}, u32[]{:S(2)}) collective-permute-start(bf16[3,128,256]{2,1,0:T(8,128)(2,1)S(1)} %get-tuple-element.97), channel_id=1, source_target_pairs={{0,8},{4,12},{8,0},{12,4},{1,9},{5,13},{9,1},{13,5},{2,10},{6,14},... | collective-permute-start | bytes 589832 | tf_op jit(solution)/shard_map/proj0_y/ppermute | solution.py:103
  12.2 8.2 %collective-permute-start.7 = (bf16[128,1024]{1,0:T(8,128)(2,1)S(1)}, bf16[128,1024]{1,0:T(8,128)(2,1)S(1)}, u32[]{:S(2)}, u32[]{:S(2)}) collective-permute-start(bf16[128,1024]{1,0:T(8,128)(2,1)S(1)} %collective-permute-done.3.refs_1_), channel_id=1, source_target_pairs={{0,2},{2,3},{3,1},{1,0},{4,6},{6,7},{7,5},{5,4},{8,10},{10,11},{11... | collective-permute-start | bytes 786440 | tf_op jit(solution)/shard_map/x2/ppermute | solution.py:112
  14.5 1.5 %collective-permute-start.4 = (bf16[3,128,256]{2,1,0:T(8,128)(2,1)S(1)}, bf16[3,128,256]{2,1,0:T(8,128)(2,1)S(1)}, u32[]{:S(2)}, u32[]{:S(2)}) collective-permute-start(bf16[3,128,256]{2,1,0:T(8,128)(2,1)S(1)} %get-tuple-element.101), channel_id=1, source_target_pairs={{0,4},{4,0},{8,12},{12,8},{1,5},{5,1},{9,13},{13,9},{2,6},{6,2},{1... | collective-permute-start | bytes 589832 | tf_op jit(solution)/shard_map/proj1_core0/ppermute | solution.py:103
  14.6 1.7 %collective-permute-start.5 = (bf16[3,128,256]{2,1,0:T(8,128)(2,1)S(1)}, bf16[3,128,256]{2,1,0:T(8,128)(2,1)S(1)}, u32[]{:S(2)}, u32[]{:S(2)}) collective-permute-start(bf16[3,128,256]{2,1,0:T(8,128)(2,1)S(1)} %get-tuple-element.103), channel_id=1, source_target_pairs={{0,4},{4,0},{8,12},{12,8},{1,5},{5,1},{9,13},{13,9},{2,6},{6,2},{1... | collective-permute-start | bytes 589832 | tf_op jit(solution)/shard_map/proj1_core1/ppermute | solution.py:103
  16.3 9.0 %collective-permute-start.6 = (bf16[3,128,256]{2,1,0:T(8,128)(2,1)S(1)}, bf16[3,128,256]{2,1,0:T(8,128)(2,1)S(1)}, u32[]{:S(2)}, u32[]{:S(2)}) collective-permute-start(bf16[3,128,256]{2,1,0:T(8,128)(2,1)S(1)} %get-tuple-element.105), channel_id=1, source_target_pairs={{0,8},{4,12},{8,0},{12,4},{1,9},{5,13},{9,1},{13,5},{2,10},{6,14},... | collective-permute-start | bytes 589832 | tf_op jit(solution)/shard_map/proj1_y/ppermute | solution.py:103
  18.1 18.2 %collective-permute-start.17 = (bf16[1024,256]{1,0:T(8,128)(2,1)S(1)}, bf16[1024,256]{1,0:T(8,128)(2,1)S(1)}, u32[]{:S(2)}, u32[]{:S(2)}) collective-permute-start(bf16[1024,256]{1,0:T(8,128)(2,1)S(1)} %get-tuple-element.130.refs_1_), channel_id=1, source_target_pairs={{0,16},{16,0},{1,17},{17,1},{2,18},{18,2},{3,19},{19,3},{4,20},{20... | collective-permute-start | bytes 1572872 | tf_op jit(solution)/shard_map/proj1_xt_x/ppermute | solution.py:103
  20.4 7.3 %collective-permute-start.11 = (bf16[128,1024]{1,0:T(8,128)(2,1)S(1)}, bf16[128,1024]{1,0:T(8,128)(2,1)S(1)}, u32[]{:S(2)}, u32[]{:S(2)}) collective-permute-start(bf16[128,1024]{1,0:T(8,128)(2,1)S(1)} %collective-permute-done.7.refs_1_.refs_0_), channel_id=1, source_target_pairs={{0,2},{2,3},{3,1},{1,0},{4,6},{6,7},{7,5},{5,4},{8,10},{10,11},{11... | collective-permute-start | bytes 786440 | tf_op jit(solution)/shard_map/x3/ppermute | solution.py:112
  23.4 1.5 %collective-permute-start.8 = (bf16[3,128,256]{2,1,0:T(8,128)(2,1)S(1)}, bf16[3,128,256]{2,1,0:T(8,128)(2,1)S(1)}, u32[]{:S(2)}, u32[]{:S(2)}) collective-permute-start(bf16[3,128,256]{2,1,0:T(8,128)(2,1)S(1)} %get-tuple-element.110), channel_id=1, source_target_pairs={{0,4},{4,0},{8,12},{12,8},{1,5},{5,1},{9,13},{13,9},{2,6},{6,2},{1... | collective-permute-start | bytes 589832 | tf_op jit(solution)/shard_map/proj2_core0/ppermute | solution.py:103
  23.5 1.7 %collective-permute-start.9 = (bf16[3,128,256]{2,1,0:T(8,128)(2,1)S(1)}, bf16[3,128,256]{2,1,0:T(8,128)(2,1)S(1)}, u32[]{:S(2)}, u32[]{:S(2)}) collective-permute-start(bf16[3,128,256]{2,1,0:T(8,128)(2,1)S(1)} %get-tuple-element.112), channel_id=1, source_target_pairs={{0,4},{4,0},{8,12},{12,8},{1,5},{5,1},{9,13},{13,9},{2,6},{6,2},{1... | collective-permute-start | bytes 589832 | tf_op jit(solution)/shard_map/proj2_core1/ppermute | solution.py:103
  25.4 3.4 %collective-permute-start.15 = (bf16[2,128,256]{2,1,0:T(8,128)(2,1)S(1)}, bf16[2,128,256]{2,1,0:T(8,128)(2,1)S(1)}, u32[]{:S(2)}, u32[]{:S(2)}) collective-permute-start(bf16[2,128,256]{2,1,0:T(8,128)(2,1)S(1)} %get-tuple-element.127), channel_id=1, source_target_pairs={{0,4},{4,0},{8,12},{12,8},{1,5},{5,1},{9,13},{13,9},{2,6},{6,2},{1... | collective-permute-start | bytes 393224 | tf_op jit(solution)/shard_map/up_core/ppermute | solution.py:103
  25.7 10.6 %collective-permute-start.10 = (bf16[3,128,256]{2,1,0:T(8,128)(2,1)S(1)}, bf16[3,128,256]{2,1,0:T(8,128)(2,1)S(1)}, u32[]{:S(2)}, u32[]{:S(2)}) collective-permute-start(bf16[3,128,256]{2,1,0:T(8,128)(2,1)S(1)} %get-tuple-element.114), channel_id=1, source_target_pairs={{0,8},{4,12},{8,0},{12,4},{1,9},{5,13},{9,1},{13,5},{2,10},{6,14},... | collective-permute-start | bytes 589832 | tf_op jit(solution)/shard_map/proj2_y/ppermute | solution.py:103
  28.3 2.0 %collective-permute-start.12 = (bf16[3,128,256]{2,1,0:T(8,128)(2,1)S(1)}, bf16[3,128,256]{2,1,0:T(8,128)(2,1)S(1)}, u32[]{:S(2)}, u32[]{:S(2)}) collective-permute-start(bf16[3,128,256]{2,1,0:T(8,128)(2,1)S(1)} %get-tuple-element.121), channel_id=1, source_target_pairs={{0,4},{4,0},{8,12},{12,8},{1,5},{5,1},{9,13},{13,9},{2,6},{6,2},{1... | collective-permute-start | bytes 589832 | tf_op jit(solution)/shard_map/proj3_core0/ppermute | solution.py:103
  28.4 3.3 %collective-permute-start.13 = (bf16[3,128,256]{2,1,0:T(8,128)(2,1)S(1)}, bf16[3,128,256]{2,1,0:T(8,128)(2,1)S(1)}, u32[]{:S(2)}, u32[]{:S(2)}) collective-permute-start(bf16[3,128,256]{2,1,0:T(8,128)(2,1)S(1)} %get-tuple-element.123), channel_id=1, source_target_pairs={{0,4},{4,0},{8,12},{12,8},{1,5},{5,1},{9,13},{13,9},{2,6},{6,2},{1... | collective-permute-start | bytes 589832 | tf_op jit(solution)/shard_map/proj3_core1/ppermute | solution.py:103
  28.9 7.4 %collective-permute-start.16 = (bf16[2,128,256]{2,1,0:T(8,128)(2,1)S(1)}, bf16[2,128,256]{2,1,0:T(8,128)(2,1)S(1)}, u32[]{:S(2)}, u32[]{:S(2)}) collective-permute-start(bf16[2,128,256]{2,1,0:T(8,128)(2,1)S(1)} %pad_maximum_fusion), channel_id=1, source_target_pairs={{0,8},{4,12},{8,0},{12,4},{1,9},{5,13},{9,1},{13,5},{2,10},{6,14},... | collective-permute-start | bytes 393224 | tf_op jit(solution)/shard_map/up_y/ppermute | solution.py:103
  29.6 10.6 %copy-start = (f32[3,3,1024]{2,1,0:T(4,128)S(1)}, f32[3,3,1024]{2,1,0:T(4,128)}, u32[]{:S(2)}) copy-start(f32[3,3,1024]{2,1,0:T(4,128)} %refs_3_.3) | copy-start | bytes 110596
  29.6 10.6 %copy-start.1 = (f32[7,1024]{1,0:T(8,128)S(1)}, f32[7,1024]{1,0:T(8,128)}, u32[]{:S(2)}) copy-start(f32[7,1024]{1,0:T(8,128)} %refs_4_.3) | copy-start | bytes 86020
  30.3 9.9 %collective-permute-start.18 = (bf16[1024,128]{1,0:T(8,128)(2,1)S(1)}, bf16[1024,128]{1,0:T(8,128)(2,1)S(1)}, u32[]{:S(2)}, u32[]{:S(2)}) collective-permute-start(bf16[1024,128]{1,0:T(8,128)(2,1)S(1)} %get-tuple-element.135.refs_2_), channel_id=1, source_target_pairs={{0,16},{16,0},{1,17},{17,1},{2,18},{18,2},{3,19},{19,3},{4,20},{20... | collective-permute-start | bytes 786440 | tf_op jit(solution)/shard_map/proj2_xt_x/ppermute | solution.py:103
  31.7 8.1 %collective-permute-start.14 = (bf16[3,128,256]{2,1,0:T(8,128)(2,1)S(1)}, bf16[3,128,256]{2,1,0:T(8,128)(2,1)S(1)}, u32[]{:S(2)}, u32[]{:S(2)}) collective-permute-start(bf16[3,128,256]{2,1,0:T(8,128)(2,1)S(1)} %get-tuple-element.125), channel_id=1, source_target_pairs={{0,8},{4,12},{8,0},{12,4},{1,9},{5,13},{9,1},{13,5},{2,10},{6,14},... | collective-permute-start | bytes 589832 | tf_op jit(solution)/shard_map/proj3_y/ppermute | solution.py:103
  36.4 8.8 %collective-permute-start.23 = (bf16[1024,128]{1,0:T(8,128)(2,1)S(1)}, bf16[1024,128]{1,0:T(8,128)(2,1)S(1)}, u32[]{:S(2)}, u32[]{:S(2)}) collective-permute-start(bf16[1024,128]{1,0:T(8,128)(2,1)S(1)} %get-tuple-element.142.refs_3_), channel_id=1, source_target_pairs={{0,16},{16,0},{1,17},{17,1},{2,18},{18,2},{3,19},{19,3},{4,20},{20... | collective-permute-start | bytes 786440 | tf_op jit(solution)/shard_map/proj3_xt_x/ppermute | solution.py:103
  40.8 6.3 %collective-permute-start.21 = (bf16[3,128,256]{2,1,0:T(8,128)(2,1)S(1)}, bf16[3,128,256]{2,1,0:T(8,128)(2,1)S(1)}, u32[]{:S(2)}, u32[]{:S(2)}) collective-permute-start(bf16[3,128,256]{2,1,0:T(8,128)(2,1)S(1)} %get-tuple-element.136.refs_5_), channel_id=1, source_target_pairs={{0,8},{4,12},{8,0},{12,4},{1,9},{5,13},{9,1},{13,5},{2,10},{6,14},... | collective-permute-start | bytes 589832 | tf_op jit(solution)/shard_map/g1_y/ppermute | solution.py:103
  43.2 10.0 %collective-permute-start.19 = (bf16[2,3,128,256]{3,2,1,0:T(8,128)(2,1)S(1)}, bf16[2,3,128,256]{3,2,1,0:T(8,128)(2,1)S(1)}, u32[]{:S(2)}, u32[]{:S(2)}) collective-permute-start(bf16[2,3,128,256]{3,2,1,0:T(8,128)(2,1)S(1)} %get-tuple-element.139.refs_0_), channel_id=1, source_target_pairs={{0,4},{4,0},{8,12},{12,8},{1,5},{5,1},{9,13},{13,9},{2,6},{6,2},{1... | collective-permute-start | bytes 1179656 | tf_op jit(solution)/shard_map/g30_core/ppermute | solution.py:103
  43.3 3.9 %collective-permute-start.26 = (bf16[3,128,256]{2,1,0:T(8,128)(2,1)S(1)}, bf16[3,128,256]{2,1,0:T(8,128)(2,1)S(1)}, u32[]{:S(2)}, u32[]{:S(2)}) collective-permute-start(bf16[3,128,256]{2,1,0:T(8,128)(2,1)S(1)} %get-tuple-element.140.refs_0_), channel_id=1, source_target_pairs={{0,4},{4,0},{8,12},{12,8},{1,5},{5,1},{9,13},{13,9},{2,6},{6,2},{1... | collective-permute-start | bytes 589832 | tf_op jit(solution)/shard_map/g2_core/ppermute | solution.py:103
  43.8 19.5 %collective-permute-start.25 = (bf16[4,3,128,256]{3,2,1,0:T(8,128)(2,1)S(1)}, bf16[4,3,128,256]{3,2,1,0:T(8,128)(2,1)S(1)}, u32[]{:S(2)}, u32[]{:S(2)}) collective-permute-start(bf16[4,3,128,256]{3,2,1,0:T(8,128)(2,1)S(1)} %get-tuple-element.138.refs_1_.refs_4_), channel_id=1, source_target_pairs={{0,16},{16,0},{1,17},{17,1},{2,18},{18,2},{3,19},{19,3},{4,20},{20... | collective-permute-start | bytes 2359304 | tf_op jit(solution)/shard_map/g_x/ppermute | solution.py:103
  45.2 2.6 %collective-permute-start.20 = (bf16[3,128,256]{2,1,0:T(8,128)(2,1)S(1)}, bf16[3,128,256]{2,1,0:T(8,128)(2,1)S(1)}, u32[]{:S(2)}, u32[]{:S(2)}) collective-permute-start(bf16[3,128,256]{2,1,0:T(8,128)(2,1)S(1)} %get-tuple-element.136.refs_5_), channel_id=1, source_target_pairs={{0,4},{4,0},{8,12},{12,8},{1,5},{5,1},{9,13},{13,9},{2,6},{6,2},{1... | collective-permute-start | bytes 589832 | tf_op jit(solution)/shard_map/g1_core/ppermute | solution.py:103
  47.1 1.4 %collective-permute-start.22 = (bf16[3,128,256]{2,1,0:T(8,128)(2,1)S(1)}, bf16[3,128,256]{2,1,0:T(8,128)(2,1)S(1)}, u32[]{:S(2)}, u32[]{:S(2)}) collective-permute-start(bf16[3,128,256]{2,1,0:T(8,128)(2,1)S(1)} %collective-permute-done.21.refs_2_.refs_3_.refs_8_), channel_id=1, source_target_pairs={{0,4},{4,0},{8,12},{12,8},{1,5},{5,1},{9,13},{13,9},{2,6},{6,2},{1... | collective-permute-start | bytes 589832 | tf_op jit(solution)/shard_map/gy1_core/ppermute | solution.py:103
  47.1 7.3 %collective-permute-start.27 = (bf16[3,128,256]{2,1,0:T(8,128)(2,1)S(1)}, bf16[3,128,256]{2,1,0:T(8,128)(2,1)S(1)}, u32[]{:S(2)}, u32[]{:S(2)}) collective-permute-start(bf16[3,128,256]{2,1,0:T(8,128)(2,1)S(1)} %get-tuple-element.146), channel_id=1, source_target_pairs={{0,8},{4,12},{8,0},{12,4},{1,9},{5,13},{9,1},{13,5},{2,10},{6,14},... | collective-permute-start | bytes 589832 | tf_op jit(solution)/shard_map/g2_y/ppermute | solution.py:103
  50.8 8.6 %collective-permute-start.29 = (bf16[128,1024]{1,0:T(8,128)(2,1)S(1)}, bf16[128,1024]{1,0:T(8,128)(2,1)S(1)}, u32[]{:S(2)}, u32[]{:S(2)}) collective-permute-start(bf16[128,1024]{1,0:T(8,128)(2,1)S(1)} %get-tuple-element.150), channel_id=1, source_target_pairs={{0,2},{2,3},{3,1},{1,0},{4,6},{6,7},{7,5},{5,4},{8,10},{10,11},{11... | collective-permute-start | bytes 786440 | tf_op jit(solution)/shard_map/share1/ppermute | solution.py:112
  53.2 10.9 %collective-permute-start.24 = (bf16[2,3,128,256]{3,2,1,0:T(8,128)(2,1)S(1)}, bf16[2,3,128,256]{3,2,1,0:T(8,128)(2,1)S(1)}, u32[]{:S(2)}, u32[]{:S(2)}) collective-permute-start(bf16[2,3,128,256]{3,2,1,0:T(8,128)(2,1)S(1)} %get-tuple-element.145), channel_id=1, source_target_pairs={{0,8},{4,12},{8,0},{12,4},{1,9},{5,13},{9,1},{13,5},{2,10},{6,14},... | collective-permute-start | bytes 1179656 | tf_op jit(solution)/shard_map/g30_y/ppermute | solution.py:103
  54.5 2.0 %collective-permute-start.28 = (bf16[3,128,256]{2,1,0:T(8,128)(2,1)S(1)}, bf16[3,128,256]{2,1,0:T(8,128)(2,1)S(1)}, u32[]{:S(2)}, u32[]{:S(2)}) collective-permute-start(bf16[3,128,256]{2,1,0:T(8,128)(2,1)S(1)} %collective-permute-done.27.refs_3_.refs_9_), channel_id=1, source_target_pairs={{0,4},{4,0},{8,12},{12,8},{1,5},{5,1},{9,13},{13,9},{2,6},{6,2},{1... | collective-permute-start | bytes 589832 | tf_op jit(solution)/shard_map/gy2_core/ppermute | solution.py:103
  63.3 7.6 %collective-permute-start.32 = (bf16[4,3,128,256]{3,2,1,0:T(8,128)(2,1)S(1)}, bf16[4,3,128,256]{3,2,1,0:T(8,128)(2,1)S(1)}, u32[]{:S(2)}, u32[]{:S(2)}) collective-permute-start(bf16[4,3,128,256]{3,2,1,0:T(8,128)(2,1)S(1)} %get-tuple-element.153.refs_0_.refs_4_), channel_id=1, source_target_pairs={{0,4},{4,0},{8,12},{12,8},{1,5},{5,1},{9,13},{13,9},{2,6},{6,2},{1... | collective-permute-start | bytes 2359304 | tf_op jit(solution)/shard_map/gx_core/ppermute | solution.py:103
  64.1 4.7 %collective-permute-start.30 = (bf16[2,3,128,256]{3,2,1,0:T(8,128)(2,1)S(1)}, bf16[2,3,128,256]{3,2,1,0:T(8,128)(2,1)S(1)}, u32[]{:S(2)}, u32[]{:S(2)}) collective-permute-start(bf16[2,3,128,256]{3,2,1,0:T(8,128)(2,1)S(1)} %get-tuple-element.156.refs_3_.refs_7_), channel_id=1, source_target_pairs={{0,4},{4,0},{8,12},{12,8},{1,5},{5,1},{9,13},{13,9},{2,6},{6,2},{1... | collective-permute-start | bytes 1179656 | tf_op jit(solution)/shard_map/gy30_core/ppermute | solution.py:103
  64.1 11.5 %collective-permute-start.33 = (bf16[2,3,128,256]{3,2,1,0:T(8,128)(2,1)S(1)}, bf16[2,3,128,256]{3,2,1,0:T(8,128)(2,1)S(1)}, u32[]{:S(2)}, u32[]{:S(2)}) collective-permute-start(bf16[2,3,128,256]{3,2,1,0:T(8,128)(2,1)S(1)} %get-tuple-element.164), channel_id=1, source_target_pairs={{0,8},{4,12},{8,0},{12,4},{1,9},{5,13},{9,1},{13,5},{2,10},{6,14},... | collective-permute-start | bytes 1179656 | tf_op jit(solution)/shard_map/gx12_y/ppermute | solution.py:103
  65.3 11.2 %collective-permute-start.35 = (bf16[2,3,128,256]{3,2,1,0:T(8,128)(2,1)S(1)}, bf16[2,3,128,256]{3,2,1,0:T(8,128)(2,1)S(1)}, u32[]{:S(2)}, u32[]{:S(2)}) collective-permute-start(bf16[2,3,128,256]{3,2,1,0:T(8,128)(2,1)S(1)} %get-tuple-element.156.refs_3_.refs_7_), channel_id=1, source_target_pairs={{0,16},{16,0},{1,17},{17,1},{2,18},{18,2},{3,19},{19,3},{4,20},{20... | collective-permute-start | bytes 1179656 | tf_op jit(solution)/shard_map/gy30_x/ppermute | solution.py:103
  66.8 8.6 %collective-permute-start.31 = (bf16[128,1024]{1,0:T(8,128)(2,1)S(1)}, bf16[128,1024]{1,0:T(8,128)(2,1)S(1)}, u32[]{:S(2)}, u32[]{:S(2)}) collective-permute-start(bf16[128,1024]{1,0:T(8,128)(2,1)S(1)} %get-tuple-element.160), channel_id=1, source_target_pairs={{0,2},{2,3},{3,1},{1,0},{4,6},{6,7},{7,5},{5,4},{8,10},{10,11},{11... | collective-permute-start | bytes 786440 | tf_op jit(solution)/shard_map/share2/ppermute | solution.py:112
  76.5 2.4 %collective-permute-start.36 = (bf16[2,3,128,256]{3,2,1,0:T(8,128)(2,1)S(1)}, bf16[2,3,128,256]{3,2,1,0:T(8,128)(2,1)S(1)}, u32[]{:S(2)}, u32[]{:S(2)}) collective-permute-start(bf16[2,3,128,256]{3,2,1,0:T(8,128)(2,1)S(1)} %get-tuple-element.167.refs_10_), channel_id=1, source_target_pairs={{0,4},{4,0},{8,12},{12,8},{1,5},{5,1},{9,13},{13,9},{2,6},{6,2},{1... | collective-permute-start | bytes 1179656 | tf_op jit(solution)/shard_map/gxy30_core/ppermute | solution.py:103
  76.5 2.4 %collective-permute-start.37 = (bf16[2,3,128,256]{3,2,1,0:T(8,128)(2,1)S(1)}, bf16[2,3,128,256]{3,2,1,0:T(8,128)(2,1)S(1)}, u32[]{:S(2)}, u32[]{:S(2)}) collective-permute-start(bf16[2,3,128,256]{3,2,1,0:T(8,128)(2,1)S(1)} %get-tuple-element.168.refs_11_), channel_id=1, source_target_pairs={{0,4},{4,0},{8,12},{12,8},{1,5},{5,1},{9,13},{13,9},{2,6},{6,2},{1... | collective-permute-start | bytes 1179656 | tf_op jit(solution)/shard_map/gxy12_core/ppermute | solution.py:103
  77.0 8.2 %collective-permute-start.34 = (bf16[128,1024]{1,0:T(8,128)(2,1)S(1)}, bf16[128,1024]{1,0:T(8,128)(2,1)S(1)}, u32[]{:S(2)}, u32[]{:S(2)}) collective-permute-start(bf16[128,1024]{1,0:T(8,128)(2,1)S(1)} %get-tuple-element.165), channel_id=1, source_target_pairs={{0,2},{2,3},{3,1},{1,0},{4,6},{6,7},{7,5},{5,4},{8,10},{10,11},{11... | collective-permute-start | bytes 786440 | tf_op jit(solution)/shard_map/share3/ppermute | solution.py:112

commit v2 on v1

--- a/solution.py
+++ b/solution.py
@@ -393,7 +393,9 @@
     return me, out
 
 
-def weight_grads(me, done, xts, blocks, width, begun=None, final=True):
+def weight_grads(me, done, xts, blocks, width, begun=None, final=True, micros=4.0):
+    cols = [x[1] if isinstance(x, tuple) else (0, x.shape[1]) for x in xts]
+    xts = [x[0] if isinstance(x, tuple) else x for x in xts]
     depth = xts[0].shape[0]
     flat = [p for _, pieces in blocks for p in pieces]
     parts, high, block = flat[0][0].shape[-3:]
@@ -412,9 +414,9 @@
         x_refs, g_refs = refs[: len(xts)], refs[len(xts) : n_in]
         out_ref, xt, gs, *rest = refs[n_in:]
         at = 0
-        for x in x_refs:
-            xt[:, at : at + x.shape[1]] = x[...]
-            at += x.shape[1]
+        for x, (low, end) in zip(x_refs, cols):
+            xt[:, at : at + end - low] = x[:, low:end]
+            at += end - low
         row = me_ref[0]
         start = pl.multiple_of((row ^ blocks[0][0]) // CORES * wide, wide)
         copies = []
@@ -470,7 +472,7 @@
         body,
         [out],
         ins,
-        (6.0 if done is not None else 0.3) if final else 4.0,
+        (6.0 if done is not None else 0.3) if final else micros,
         specs,
         scratch=scratch,
         out_specs=[ANY if final else VMEM],
@@ -589,6 +591,10 @@
     with jax.named_scope("total2"):
         me, share2 = total(me, [share2, passed])
     passed = send("share2", share2, "col", 1)
+    far_own = [(2, [(y1, None), (y2, None)]), (3, [(cy1, None), (cy2, None)])]
+    with jax.named_scope("weight_grads_far_own"):
+        some = [(xts[0], (high, 2 * high)), xts[1]]
+        me, far_begun = weight_grads(me, None, some, far_own, width, final=False, micros=0.05)
     with jax.named_scope("relay_x"):
         me, (x,) = relay(me, x)
     with jax.named_scope("first_half"):
@@ -611,10 +617,12 @@
     cxy12, cxy30 = send("gxy12_core", xy12, "row", 1), send("gxy30_core", xy30, "row", 1)
     with jax.named_scope("weight_grads_far"):
         blocks = [
-            (2, cut(y30, y1, y2) + halves(xy12, xy30)),
-            (3, cut(cy30, cy1, cy2) + halves(cxy12, cxy30)),
+            (2, [(y30, 1), (y30, 0)] + halves(xy12, xy30)),
+            (3, [(cy30, 1), (cy30, 0)] + halves(cxy12, cxy30)),
         ]
-        me, grad_w = weight_grads(me, grad_w, xts + others, blocks, width)
+        me, grad_w = weight_grads(
+            me, grad_w, [(xts[0], (0, high)), xts[2], *others], blocks, width, far_begun
+        )
     with jax.named_scope("total0"):
         me, grad_in = total(me, [share0, passed])
     return (grad_in[None], jnp.transpose(grad_w, (1, 0, 2)))

time: 86.1 us -> 86.1 us (level)
    ppermute x32, waiting for transfers between devices: 15 us -> 13.9 us  [swap(): return lax.ppermute(value, axis, [(i, i ^ step) for i in range(size)])]
    ppermute x6, waiting for transfers between devices: 2.86 us -> 3.78 us  [along(): return lax.ppermute(value, 'col', pairs)]
    pallas_call x34 -> x35, Pallas kernels: 31.4 us -> 31.6 us  [local(): pl.pallas_call(ordered, out_shape=[jax.ShapeDtypeStruct((8, LANES), jnp.f...]
where the time goes in v2:
time: 86.1 us; the launch traced here: 86 us
  starting transfers between devices  35.6 us (41%)
  Pallas kernels  31.6 us (37%)
  waiting for transfers between devices  17.7 us (21%)
  between operations  0.97 us (1%)
    pallas_call x35, Pallas kernels, local(): pl.pallas_call(ordered, out_shape=[jax.ShapeDtypeStruct((8, LANES), jnp.f...  31.6 us
    ppermute x32, starting transfers between devices, swap(): return lax.ppermute(value, axis, [(i, i ^ step) for i in range(size)])  21 us
    ppermute x6, starting transfers between devices, along(): return lax.ppermute(value, 'col', pairs)  14.6 us
    ppermute x32, waiting for transfers between devices, swap(): return lax.ppermute(value, axis, [(i, i ^ step) for i in range(size)])  13.9 us
    ppermute x6, waiting for transfers between devices, along(): return lax.ppermute(value, 'col', pairs)  3.78 us
  transfers between devices with their start and end apart: 38, of which 19 were waited for; matrix products, arithmetic and copies ran while one was open for 0% of the time, Pallas kernels for 36%

profile of v2, /device:TPU:0, one launch (start us, length us, event | category | flops | bytes accessed | tf_op | source)
XLA Modules:
  0.0 86.0 jit_solution(15977903840156773267)
XLA Ops:
  0.6 4.1 %collective-permute-start.3 = (bf16[128,1024]{1,0:T(8,128)(2,1)}, bf16[128,1024]{1,0:T(8,128)(2,1)S(1)}, u32[]{:S(2)}, u32[]{:S(2)}) collective-permute-start(bf16[128,1024]{1,0:T(8,128)(2,1)} %bitcast.18), channel_id=1, source_target_pairs={{0,2},{2,3},{3,1},{1,0},{4,6},{6,7},{7,5},{5,4},{8,10},{10,11},{11... | collective-permute-start | bytes 786440 | tf_op jit(solution)/shard_map/x1/ppermute | solution.py:112
  4.8 4.0 %begin.1 = (f32[8,128]{1,0:T(8,128)S(1)}, bf16[3,1024,1024]{2,1,0:T(8,128)(2,1)S(1)}, bf16[128,1024]{1,0:T(8,128)(2,1)S(1)}, bf16[2,128,256]{2,1,0:T(8,128)(2,1)...) custom-call(s32[2]{0:T(128)S(1)} %pad_add_fusion.refs_0_, ...), custom_call_target="tpu_custom_call" | custom-call | flops 3849999872 | bytes 1 | tf_op jit(solution)/shard_map/begin/pallas_call | solution.py:151
  8.8 0.5 collective-permute-start.1
  9.3 0.6 proj0_keep.1
  10.0 0.3 collective-permute-done.refs_3_.refs_2_
  10.3 0.3 collective-permute-done.1.refs_1_
  10.6 1.6 %collective-permute-start.2 = (bf16[3,128,256]{2,1,0:T(8,128)(2,1)S(1)}, bf16[3,128,256]{2,1,0:T(8,128)(2,1)S(1)}, u32[]{:S(2)}, u32[]{:S(2)}) collective-permute-start(bf16[3,128,256]{2,1,0:T(8,128)(2,1)S(1)} %get-tuple-element.99), channel_id=1, source_target_pairs={{0,8},{4,12},{8,0},{12,4},{1,9},{5,13},{9,1},{13,5},{2,10},{6,14},... | collective-permute-start | bytes 589832 | tf_op jit(solution)/shard_map/proj0_y/ppermute | solution.py:103
  12.2 1.7 %collective-permute-start.7 = (bf16[128,1024]{1,0:T(8,128)(2,1)S(1)}, bf16[128,1024]{1,0:T(8,128)(2,1)S(1)}, u32[]{:S(2)}, u32[]{:S(2)}) collective-permute-start(bf16[128,1024]{1,0:T(8,128)(2,1)S(1)} %collective-permute-done.3.refs_1_), channel_id=1, source_target_pairs={{0,2},{2,3},{3,1},{1,0},{4,6},{6,7},{7,5},{5,4},{8,10},{10,11},{11... | collective-permute-start | bytes 786440 | tf_op jit(solution)/shard_map/x2/ppermute | solution.py:112
  13.9 0.6 proj1_away.1
  14.6 0.5 collective-permute-start.5
  15.1 0.6 proj1_keep.1
  15.7 0.3 collective-permute-done.4.refs_3_.refs_5_
  16.0 0.3 collective-permute-done.5.refs_1_
  16.3 1.6 %collective-permute-start.6 = (bf16[3,128,256]{2,1,0:T(8,128)(2,1)S(1)}, bf16[3,128,256]{2,1,0:T(8,128)(2,1)S(1)}, u32[]{:S(2)}, u32[]{:S(2)}) collective-permute-start(bf16[3,128,256]{2,1,0:T(8,128)(2,1)S(1)} %get-tuple-element.107), channel_id=1, source_target_pairs={{0,8},{4,12},{8,0},{12,4},{1,9},{5,13},{9,1},{13,5},{2,10},{6,14},... | collective-permute-start | bytes 589832 | tf_op jit(solution)/shard_map/proj1_y/ppermute | solution.py:103
  18.1 1.6 %collective-permute-start.17 = (bf16[1024,256]{1,0:T(8,128)(2,1)S(1)}, bf16[1024,256]{1,0:T(8,128)(2,1)S(1)}, u32[]{:S(2)}, u32[]{:S(2)}) collective-permute-start(bf16[1024,256]{1,0:T(8,128)(2,1)S(1)} %get-tuple-element.132.refs_1_), channel_id=1, source_target_pairs={{0,16},{16,0},{1,17},{17,1},{2,18},{18,2},{3,19},{19,3},{4,20},{20... | collective-permute-start | bytes 1572872 | tf_op jit(solution)/shard_map/proj1_xt_x/ppermute | solution.py:103
  19.7 0.7 collective-permute-done.7.refs_1_.refs_0_
  20.4 2.5 %collective-permute-start.11 = (bf16[128,1024]{1,0:T(8,128)(2,1)S(1)}, bf16[128,1024]{1,0:T(8,128)(2,1)S(1)}, u32[]{:S(2)}, u32[]{:S(2)}) collective-permute-start(bf16[128,1024]{1,0:T(8,128)(2,1)S(1)} %collective-permute-done.7.refs_1_.refs_0_), channel_id=1, source_target_pairs={{0,2},{2,3},{3,1},{1,0},{4,6},{6,7},{7,5},{5,4},{8,10},{10,11},{11... | collective-permute-start | bytes 786440 | tf_op jit(solution)/shard_map/x3/ppermute | solution.py:112
  22.8 0.6 proj2_away.1
  23.5 0.5 collective-permute-start.9
  24.0 0.6 proj2_keep.1
  24.6 0.3 collective-permute-done.8.refs_3_.refs_8_
  24.9 0.3 collective-permute-done.9.refs_1_
  25.4 0.3 collective-permute-start.15
  25.7 0.6 collective-permute-start.10
  26.4 1.3 %collective-permute-done.11.refs_1_.refs_0_ = bf16[128,1024]{1,0:T(8,128)(2,1)S(1)} collective-permute-done((bf16[128,1024]{1,0:T(8,128)(2,1)S(1)}, bf16[128,1024]{1,0:T(8,128)(2,1)S(1)}, u32[]{:S(2)}, u32[]{:S(2)}) %collective-permute-start.11) | collective-permute-done | bytes 262176 | tf_op jit(solution)/shard_map/x3/ppermute | solution.py:112
  27.7 0.6 proj3_away.1
  28.4 0.5 collective-permute-start.13
  28.9 0.7 collective-permute-start.16
  29.6 0.6 proj3_keep.1
  30.3 1.4 %collective-permute-start.18 = (bf16[1024,128]{1,0:T(8,128)(2,1)S(1)}, bf16[1024,128]{1,0:T(8,128)(2,1)S(1)}, u32[]{:S(2)}, u32[]{:S(2)}) collective-permute-start(bf16[1024,128]{1,0:T(8,128)(2,1)S(1)} %get-tuple-element.137.refs_2_), channel_id=1, source_target_pairs={{0,16},{16,0},{1,17},{17,1},{2,18},{18,2},{3,19},{19,3},{4,20},{20... | collective-permute-start | bytes 786440 | tf_op jit(solution)/shard_map/proj2_xt_x/ppermute | solution.py:103
  31.7 1.6 %collective-permute-start.14 = (bf16[3,128,256]{2,1,0:T(8,128)(2,1)S(1)}, bf16[3,128,256]{2,1,0:T(8,128)(2,1)S(1)}, u32[]{:S(2)}, u32[]{:S(2)}) collective-permute-start(bf16[3,128,256]{2,1,0:T(8,128)(2,1)S(1)} %get-tuple-element.127), channel_id=1, source_target_pairs={{0,8},{4,12},{8,0},{12,4},{1,9},{5,13},{9,1},{13,5},{2,10},{6,14},... | collective-permute-start | bytes 589832 | tf_op jit(solution)/shard_map/proj3_y/ppermute | solution.py:103
  33.3 3.0 %collective-permute-done.16 = bf16[2,128,256]{2,1,0:T(8,128)(2,1)S(1)} collective-permute-done((bf16[2,128,256]{2,1,0:T(8,128)(2,1)S(1)}, bf16[2,128,256]{2,1,0:T(8,128)(2,1)S(1)}, u32[]{:S(2)}, u32[]{:S(2)}) %collective-permute-start.16) | collective-permute-done | bytes 131104 | tf_op jit(solution)/shard_map/up_y/ppermute | solution.py:103
  36.4 1.6 %collective-permute-start.23 = (bf16[1024,128]{1,0:T(8,128)(2,1)S(1)}, bf16[1024,128]{1,0:T(8,128)(2,1)S(1)}, u32[]{:S(2)}, u32[]{:S(2)}) collective-permute-start(bf16[1024,128]{1,0:T(8,128)(2,1)S(1)} %get-tuple-element.144.refs_3_.refs_2_), channel_id=1, source_target_pairs={{0,16},{16,0},{1,17},{17,1},{2,18},{18,2},{3,19},{19,3},{4,20},{20... | collective-permute-start | bytes 786440 | tf_op jit(solution)/shard_map/proj3_xt_x/ppermute | solution.py:103
  38.0 1.9 %collective-permute-done.14.refs_12_ = bf16[3,128,256]{2,1,0:T(8,128)(2,1)S(1)} collective-permute-done((bf16[3,128,256]{2,1,0:T(8,128)(2,1)S(1)}, bf16[3,128,256]{2,1,0:T(8,128)(2,1)S(1)}, u32[]{:S(2)}, u32[]{:S(2)}) %collective-permute-start.14) | collective-permute-done | bytes 196640 | tf_op jit(solution)/shard_map/proj3_y/ppermute | solution.py:103
  39.8 0.4 laid_out.1
  40.2 0.6 gate1.1
  40.8 0.7 collective-permute-start.21
  41.5 1.7 %gate230.1 = (f32[8,128]{1,0:T(8,128)S(1)}, bf16[4,3,128,256]{3,2,1,0:T(8,128)(2,1)S(1)}, bf16[2,3,128,256]{3,2,1,0:T(8,128)(2,1)S(1)}, bf16[3,128,256]{2,1,0:T(8,128)(2,1)S(1)}) custom-call(s32[2]{0:T(128)S(4)} %get-tuple-element.90.refs_0_, f32[3,528,256]{2,1,0:T(8,128)S(1)} %get-tuple-element.134.refs_1_, ...), custom_call_target="tpu_custom_call", output_to_operand_aliasing={{0}: (6, {})} | custom-call | flops 2640000000 | bytes 1 | tf_op jit(solution)/shard_map/gate230/pallas_call | solution.py:151
  43.3 0.5 collective-permute-start.28
  43.8 1.5 %collective-permute-start.25 = (bf16[4,3,128,256]{3,2,1,0:T(8,128)(2,1)S(1)}, bf16[4,3,128,256]{3,2,1,0:T(8,128)(2,1)S(1)}, u32[]{:S(2)}, u32[]{:S(2)}) collective-permute-start(bf16[4,3,128,256]{3,2,1,0:T(8,128)(2,1)S(1)} %get-tuple-element.140.refs_1_.refs_4_), channel_id=1, source_target_pairs={{0,16},{16,0},{1,17},{17,1},{2,18},{18,2},{3,19},{19,3},{4,20},{20... | collective-permute-start | bytes 2359304 | tf_op jit(solution)/shard_map/g_x/ppermute | solution.py:103
  45.3 1.9 %collective-permute-done.21.refs_2_.refs_3_ = bf16[3,128,256]{2,1,0:T(8,128)(2,1)S(1)} collective-permute-done((bf16[3,128,256]{2,1,0:T(8,128)(2,1)S(1)}, bf16[3,128,256]{2,1,0:T(8,128)(2,1)S(1)}, u32[]{:S(2)}, u32[]{:S(2)}) %collective-permute-start.21) | collective-permute-done | bytes 196640 | tf_op jit(solution)/shard_map/g1_y/ppermute | solution.py:103
  47.2 0.7 collective-permute-start.26
  47.9 0.7 collective-permute-done.22.refs_4_.refs_5_
  48.6 2.2 %input_grads1.1 = (f32[8,128]{1,0:T(8,128)S(1)}, bf16[128,1024]{1,0:T(8,128)(2,1)S(1)}) custom-call(s32[2]{0:T(128)S(4)} %get-tuple-element.90.refs_0_, bf16[4,3,128,256]{3,2,1,0:T(8,128)(2,1)S(1)} %get-tuple-element.140.refs_1_.refs_4_, bf16[3,128,256]{2,1,0:T(8,128)(2,1)S(1)} %collective-permute-done.20.refs_2_.refs_6_, ...), custom_call_target="tpu_custom_call", output_to_operand_aliasing={{0}: (6, {})} | custom-call | flops 880000000 | bytes 1 | tf_op jit(solution)/shard_map/input_grads1/pallas_call | solution.py:151
  50.8 2.4 %collective-permute-start.29 = (bf16[128,1024]{1,0:T(8,128)(2,1)S(1)}, bf16[128,1024]{1,0:T(8,128)(2,1)S(1)}, u32[]{:S(2)}, u32[]{:S(2)}) collective-permute-start(bf16[128,1024]{1,0:T(8,128)(2,1)S(1)} %get-tuple-element.152), channel_id=1, source_target_pairs={{0,2},{2,3},{3,1},{1,0},{4,6},{6,7},{7,5},{5,4},{8,10},{10,11},{11... | collective-permute-start | bytes 786440 | tf_op jit(solution)/shard_map/share1/ppermute | solution.py:112
  53.2 1.1 %collective-permute-start.24 = (bf16[2,3,128,256]{3,2,1,0:T(8,128)(2,1)S(1)}, bf16[2,3,128,256]{3,2,1,0:T(8,128)(2,1)S(1)}, u32[]{:S(2)}, u32[]{:S(2)}) collective-permute-start(bf16[2,3,128,256]{3,2,1,0:T(8,128)(2,1)S(1)} %get-tuple-element.147), channel_id=1, source_target_pairs={{0,8},{4,12},{8,0},{12,4},{1,9},{5,13},{9,1},{13,5},{2,10},{6,14},... | collective-permute-start | bytes 1179656 | tf_op jit(solution)/shard_map/g30_y/ppermute | solution.py:103
  54.5 2.0 %weight_grads_near_own.1 = (f32[8,128]{1,0:T(8,128)S(1)}, f32[3,1024,512]{2,1,0:T(8,128)S(1)}) custom-call(s32[2]{0:T(128)S(4)} %get-tuple-element.90.refs_0_, bf16[1024,256]{1,0:T(8,128)(2,1)S(1)} %get-tuple-element.132.refs_1_, bf16[1024,128]{1,0:T(8,128)(2,1)S(1)} %get-tuple-element.137.refs_2_, ...), custom_call_target="tpu_custom_call", output_to_operand_aliasing={{0}: (8, {})} | custom-call | flops 4400000000 | bytes 1 | tf_op jit(solution)/shard_map/weight_grads_near_own/pallas_call | solution.py:151
  56.5 2.2 %input_grads2.1 = (f32[8,128]{1,0:T(8,128)S(1)}, bf16[128,1024]{1,0:T(8,128)(2,1)S(1)}) custom-call(s32[2]{0:T(128)S(4)} %get-tuple-element.90.refs_0_, bf16[4,3,128,256]{3,2,1,0:T(8,128)(2,1)S(1)} %get-tuple-element.140.refs_1_.refs_4_, bf16[3,128,256]{2,1,0:T(8,128)(2,1)S(1)} %collective-permute-done.28.refs_7_.refs_2_, ...), custom_call_target="tpu_custom_call", output_to_operand_aliasing={{0}: (6, {})} | custom-call | flops 880000000 | bytes 1 | tf_op jit(solution)/shard_map/input_grads2/pallas_call | solution.py:151
  58.7 0.7 collective-permute-done.29.refs_1_
  59.5 1.1 %weight_grads_far_own.1 = (f32[8,128]{1,0:T(8,128)S(1)}, f32[3,1024,512]{2,1,0:T(8,128)S(1)}) custom-call(s32[2]{0:T(128)S(4)} %get-tuple-element.90.refs_0_, bf16[1024,256]{1,0:T(8,128)(2,1)S(1)} %get-tuple-element.132.refs_1_, bf16[1024,128]{1,0:T(8,128)(2,1)S(1)} %get-tuple-element.137.refs_2_, ...), custom_call_target="tpu_custom_call", output_to_operand_aliasing={{0}: (7, {})} | custom-call | flops 55000000 | bytes 1 | tf_op jit(solution)/shard_map/weight_grads_far_own/pallas_call | solution.py:151
  60.6 2.7 %collective-permute-done.25.refs_0_ = bf16[4,3,128,256]{3,2,1,0:T(8,128)(2,1)S(1)} collective-permute-done((bf16[4,3,128,256]{3,2,1,0:T(8,128)(2,1)S(1)}, bf16[4,3,128,256]{3,2,1,0:T(8,128)(2,1)S(1)}, u32[]{:S(2)}, u32[]{:S(2)}) %collective-permute-start.25) | collective-permute-done | bytes 786464 | tf_op jit(solution)/shard_map/g_x/ppermute | solution.py:103
  63.3 0.8 collective-permute-done.24.refs_0_
  64.1 1.2 %collective-permute-start.33 = (bf16[2,3,128,256]{3,2,1,0:T(8,128)(2,1)S(1)}, bf16[2,3,128,256]{3,2,1,0:T(8,128)(2,1)S(1)}, u32[]{:S(2)}, u32[]{:S(2)}) collective-permute-start(bf16[2,3,128,256]{3,2,1,0:T(8,128)(2,1)S(1)} %get-tuple-element.167), channel_id=1, source_target_pairs={{0,8},{4,12},{8,0},{12,4},{1,9},{5,13},{9,1},{13,5},{2,10},{6,14},... | collective-permute-start | bytes 1179656 | tf_op jit(solution)/shard_map/gx12_y/ppermute | solution.py:103
  65.3 1.5 %collective-permute-start.35 = (bf16[2,3,128,256]{3,2,1,0:T(8,128)(2,1)S(1)}, bf16[2,3,128,256]{3,2,1,0:T(8,128)(2,1)S(1)}, u32[]{:S(2)}, u32[]{:S(2)}) collective-permute-start(bf16[2,3,128,256]{3,2,1,0:T(8,128)(2,1)S(1)} %get-tuple-element.159.refs_3_.refs_6_), channel_id=1, source_target_pairs={{0,16},{16,0},{1,17},{17,1},{2,18},{18,2},{3,19},{19,3},{4,20},{20... | collective-permute-start | bytes 1179656 | tf_op jit(solution)/shard_map/gy30_x/ppermute | solution.py:103
  66.8 2.1 %collective-permute-start.31 = (bf16[128,1024]{1,0:T(8,128)(2,1)S(1)}, bf16[128,1024]{1,0:T(8,128)(2,1)S(1)}, u32[]{:S(2)}, u32[]{:S(2)}) collective-permute-start(bf16[128,1024]{1,0:T(8,128)(2,1)S(1)} %get-tuple-element.163), channel_id=1, source_target_pairs={{0,2},{2,3},{3,1},{1,0},{4,6},{6,7},{7,5},{5,4},{8,10},{10,11},{11... | collective-permute-start | bytes 786440 | tf_op jit(solution)/shard_map/share2/ppermute | solution.py:112
  68.9 2.0 %input_grads30.1 = (f32[8,128]{1,0:T(8,128)S(1)}, bf16[128,1024]{1,0:T(8,128)(2,1)S(1)}, bf16[128,1024]{1,0:T(8,128)(2,1)S(1)}) custom-call(s32[2]{0:T(128)S(4)} %get-tuple-element.90.refs_0_, bf16[4,3,128,256]{3,2,1,0:T(8,128)(2,1)S(1)} %get-tuple-element.140.refs_1_.refs_4_, ...), custom_call_target="tpu_custom_call", output_to_operand_aliasing={{0}: (6, {})} | custom-call | flops 330000000 | bytes 1 | tf_op jit(solution)/shard_map/input_grads30/pallas_call | solution.py:151
  70.9 4.5 %weight_grads_near.1 = (f32[8,128]{1,0:T(8,128)S(1)}, f32[3,1024,1024]{2,1,0:T(8,128)}) custom-call(s32[2]{0:T(128)S(4)} %get-tuple-element.90.refs_0_, bf16[1024,256]{1,0:T(8,128)(2,1)S(1)} %collective-permute-done.17.refs_3_.refs_1_, bf16[1024,128]{1,0:T(8,128)(2,1)S(1)} %collective-permute-done.18.refs_6_.refs_2_.refs_4_, ...), custom_call_target="tpu_custom_call", output_to_operand_aliasing={{0}: (7, {})} | custom-call | flops 330000000 | bytes 1 | tf_op jit(solution)/shard_map/weight_grads_near/pallas_call | solution.py:151
  75.4 0.3 collective-permute-done.33.refs_3_.refs_0_
  75.7 0.8 collective-permute-done.35.refs_1_
  76.5 0.5 collective-permute-start.37
  77.0 1.9 %collective-permute-start.34 = (bf16[128,1024]{1,0:T(8,128)(2,1)S(1)}, bf16[128,1024]{1,0:T(8,128)(2,1)S(1)}, u32[]{:S(2)}, u32[]{:S(2)}) collective-permute-start(bf16[128,1024]{1,0:T(8,128)(2,1)S(1)} %get-tuple-element.168), channel_id=1, source_target_pairs={{0,2},{2,3},{3,1},{1,0},{4,6},{6,7},{7,5},{5,4},{8,10},{10,11},{11... | collective-permute-start | bytes 786440 | tf_op jit(solution)/shard_map/share3/ppermute | solution.py:112
  78.9 5.2 %weight_grads_far.1 = (f32[8,128]{1,0:T(8,128)S(1)}, f32[3,1024,1024]{2,1,0:T(8,128)}) custom-call(s32[2]{0:T(128)S(4)} %get-tuple-element.90.refs_0_, bf16[1024,256]{1,0:T(8,128)(2,1)S(1)} %get-tuple-element.132.refs_1_, bf16[1024,128]{1,0:T(8,128)(2,1)S(1)} %get-tuple-element.144.refs_3_.refs_2_, ...), custom_call_target="tpu_custom_call", output_to_operand_aliasing={{0}: (14, {}), {1}: (13, {})} | custom-call | flops 6600000000 | bytes 1 | tf_op jit(solution)/shard_map/weight_grads_far/pallas_call | solution.py:151
  84.1 1.1 %collective-permute-done.34.refs_1_ = bf16[128,1024]{1,0:T(8,128)(2,1)S(1)} collective-permute-done((bf16[128,1024]{1,0:T(8,128)(2,1)S(1)}, bf16[128,1024]{1,0:T(8,128)(2,1)S(1)}, u32[]{:S(2)}, u32[]{:S(2)}) %collective-permute-start.34) | collective-permute-done | bytes 262176 | tf_op jit(solution)/shard_map/share3/ppermute | solution.py:112
  85.2 0.8 total0.1
  (55 shorter events, 1.4 us)
Async XLA Ops:
  0.6 11.6 %collective-permute-start.3 = (bf16[128,1024]{1,0:T(8,128)(2,1)}, bf16[128,1024]{1,0:T(8,128)(2,1)S(1)}, u32[]{:S(2)}, u32[]{:S(2)}) collective-permute-start(bf16[128,1024]{1,0:T(8,128)(2,1)} %bitcast.18), channel_id=1, source_target_pairs={{0,2},{2,3},{3,1},{1,0},{4,6},{6,7},{7,5},{5,4},{8,10},{10,11},{11... | collective-permute-start | bytes 786440 | tf_op jit(solution)/shard_map/x1/ppermute | solution.py:112
  8.8 1.5 %collective-permute-start = (bf16[3,128,256]{2,1,0:T(8,128)(2,1)S(1)}, bf16[3,128,256]{2,1,0:T(8,128)(2,1)S(1)}, u32[]{:S(2)}, u32[]{:S(2)}) collective-permute-start(bf16[3,128,256]{2,1,0:T(8,128)(2,1)S(1)} %get-tuple-element.95), channel_id=1, source_target_pairs={{0,4},{4,0},{8,12},{12,8},{1,5},{5,1},{9,13},{13,9},{2,6},{6,2},{1... | collective-permute-start | bytes 589832 | tf_op jit(solution)/shard_map/proj0_core0/ppermute | solution.py:103
  8.8 1.7 %collective-permute-start.1 = (bf16[3,128,256]{2,1,0:T(8,128)(2,1)S(1)}, bf16[3,128,256]{2,1,0:T(8,128)(2,1)S(1)}, u32[]{:S(2)}, u32[]{:S(2)}) collective-permute-start(bf16[3,128,256]{2,1,0:T(8,128)(2,1)S(1)} %get-tuple-element.97), channel_id=1, source_target_pairs={{0,4},{4,0},{8,12},{12,8},{1,5},{5,1},{9,13},{13,9},{2,6},{6,2},{1... | collective-permute-start | bytes 589832 | tf_op jit(solution)/shard_map/proj0_core1/ppermute | solution.py:103
  10.6 7.3 %collective-permute-start.2 = (bf16[3,128,256]{2,1,0:T(8,128)(2,1)S(1)}, bf16[3,128,256]{2,1,0:T(8,128)(2,1)S(1)}, u32[]{:S(2)}, u32[]{:S(2)}) collective-permute-start(bf16[3,128,256]{2,1,0:T(8,128)(2,1)S(1)} %get-tuple-element.99), channel_id=1, source_target_pairs={{0,8},{4,12},{8,0},{12,4},{1,9},{5,13},{9,1},{13,5},{2,10},{6,14},... | collective-permute-start | bytes 589832 | tf_op jit(solution)/shard_map/proj0_y/ppermute | solution.py:103
  12.2 8.2 %collective-permute-start.7 = (bf16[128,1024]{1,0:T(8,128)(2,1)S(1)}, bf16[128,1024]{1,0:T(8,128)(2,1)S(1)}, u32[]{:S(2)}, u32[]{:S(2)}) collective-permute-start(bf16[128,1024]{1,0:T(8,128)(2,1)S(1)} %collective-permute-done.3.refs_1_), channel_id=1, source_target_pairs={{0,2},{2,3},{3,1},{1,0},{4,6},{6,7},{7,5},{5,4},{8,10},{10,11},{11... | collective-permute-start | bytes 786440 | tf_op jit(solution)/shard_map/x2/ppermute | solution.py:112
  14.5 1.5 %collective-permute-start.4 = (bf16[3,128,256]{2,1,0:T(8,128)(2,1)S(1)}, bf16[3,128,256]{2,1,0:T(8,128)(2,1)S(1)}, u32[]{:S(2)}, u32[]{:S(2)}) collective-permute-start(bf16[3,128,256]{2,1,0:T(8,128)(2,1)S(1)} %get-tuple-element.103), channel_id=1, source_target_pairs={{0,4},{4,0},{8,12},{12,8},{1,5},{5,1},{9,13},{13,9},{2,6},{6,2},{1... | collective-permute-start | bytes 589832 | tf_op jit(solution)/shard_map/proj1_core0/ppermute | solution.py:103
  14.6 1.7 %collective-permute-start.5 = (bf16[3,128,256]{2,1,0:T(8,128)(2,1)S(1)}, bf16[3,128,256]{2,1,0:T(8,128)(2,1)S(1)}, u32[]{:S(2)}, u32[]{:S(2)}) collective-permute-start(bf16[3,128,256]{2,1,0:T(8,128)(2,1)S(1)} %get-tuple-element.105), channel_id=1, source_target_pairs={{0,4},{4,0},{8,12},{12,8},{1,5},{5,1},{9,13},{13,9},{2,6},{6,2},{1... | collective-permute-start | bytes 589832 | tf_op jit(solution)/shard_map/proj1_core1/ppermute | solution.py:103
  16.3 9.0 %collective-permute-start.6 = (bf16[3,128,256]{2,1,0:T(8,128)(2,1)S(1)}, bf16[3,128,256]{2,1,0:T(8,128)(2,1)S(1)}, u32[]{:S(2)}, u32[]{:S(2)}) collective-permute-start(bf16[3,128,256]{2,1,0:T(8,128)(2,1)S(1)} %get-tuple-element.107), channel_id=1, source_target_pairs={{0,8},{4,12},{8,0},{12,4},{1,9},{5,13},{9,1},{13,5},{2,10},{6,14},... | collective-permute-start | bytes 589832 | tf_op jit(solution)/shard_map/proj1_y/ppermute | solution.py:103
  18.1 18.2 %collective-permute-start.17 = (bf16[1024,256]{1,0:T(8,128)(2,1)S(1)}, bf16[1024,256]{1,0:T(8,128)(2,1)S(1)}, u32[]{:S(2)}, u32[]{:S(2)}) collective-permute-start(bf16[1024,256]{1,0:T(8,128)(2,1)S(1)} %get-tuple-element.132.refs_1_), channel_id=1, source_target_pairs={{0,16},{16,0},{1,17},{17,1},{2,18},{18,2},{3,19},{19,3},{4,20},{20... | collective-permute-start | bytes 1572872 | tf_op jit(solution)/shard_map/proj1_xt_x/ppermute | solution.py:103
  20.4 7.3 %collective-permute-start.11 = (bf16[128,1024]{1,0:T(8,128)(2,1)S(1)}, bf16[128,1024]{1,0:T(8,128)(2,1)S(1)}, u32[]{:S(2)}, u32[]{:S(2)}) collective-permute-start(bf16[128,1024]{1,0:T(8,128)(2,1)S(1)} %collective-permute-done.7.refs_1_.refs_0_), channel_id=1, source_target_pairs={{0,2},{2,3},{3,1},{1,0},{4,6},{6,7},{7,5},{5,4},{8,10},{10,11},{11... | collective-permute-start | bytes 786440 | tf_op jit(solution)/shard_map/x3/ppermute | solution.py:112
  23.4 1.5 %collective-permute-start.8 = (bf16[3,128,256]{2,1,0:T(8,128)(2,1)S(1)}, bf16[3,128,256]{2,1,0:T(8,128)(2,1)S(1)}, u32[]{:S(2)}, u32[]{:S(2)}) collective-permute-start(bf16[3,128,256]{2,1,0:T(8,128)(2,1)S(1)} %get-tuple-element.112), channel_id=1, source_target_pairs={{0,4},{4,0},{8,12},{12,8},{1,5},{5,1},{9,13},{13,9},{2,6},{6,2},{1... | collective-permute-start | bytes 589832 | tf_op jit(solution)/shard_map/proj2_core0/ppermute | solution.py:103
  23.5 1.7 %collective-permute-start.9 = (bf16[3,128,256]{2,1,0:T(8,128)(2,1)S(1)}, bf16[3,128,256]{2,1,0:T(8,128)(2,1)S(1)}, u32[]{:S(2)}, u32[]{:S(2)}) collective-permute-start(bf16[3,128,256]{2,1,0:T(8,128)(2,1)S(1)} %get-tuple-element.114), channel_id=1, source_target_pairs={{0,4},{4,0},{8,12},{12,8},{1,5},{5,1},{9,13},{13,9},{2,6},{6,2},{1... | collective-permute-start | bytes 589832 | tf_op jit(solution)/shard_map/proj2_core1/ppermute | solution.py:103
  25.4 3.4 %collective-permute-start.15 = (bf16[2,128,256]{2,1,0:T(8,128)(2,1)S(1)}, bf16[2,128,256]{2,1,0:T(8,128)(2,1)S(1)}, u32[]{:S(2)}, u32[]{:S(2)}) collective-permute-start(bf16[2,128,256]{2,1,0:T(8,128)(2,1)S(1)} %get-tuple-element.129), channel_id=1, source_target_pairs={{0,4},{4,0},{8,12},{12,8},{1,5},{5,1},{9,13},{13,9},{2,6},{6,2},{1... | collective-permute-start | bytes 393224 | tf_op jit(solution)/shard_map/up_core/ppermute | solution.py:103
  25.7 10.6 %collective-permute-start.10 = (bf16[3,128,256]{2,1,0:T(8,128)(2,1)S(1)}, bf16[3,128,256]{2,1,0:T(8,128)(2,1)S(1)}, u32[]{:S(2)}, u32[]{:S(2)}) collective-permute-start(bf16[3,128,256]{2,1,0:T(8,128)(2,1)S(1)} %get-tuple-element.116), channel_id=1, source_target_pairs={{0,8},{4,12},{8,0},{12,4},{1,9},{5,13},{9,1},{13,5},{2,10},{6,14},... | collective-permute-start | bytes 589832 | tf_op jit(solution)/shard_map/proj2_y/ppermute | solution.py:103
  28.3 2.0 %collective-permute-start.12 = (bf16[3,128,256]{2,1,0:T(8,128)(2,1)S(1)}, bf16[3,128,256]{2,1,0:T(8,128)(2,1)S(1)}, u32[]{:S(2)}, u32[]{:S(2)}) collective-permute-start(bf16[3,128,256]{2,1,0:T(8,128)(2,1)S(1)} %get-tuple-element.123), channel_id=1, source_target_pairs={{0,4},{4,0},{8,12},{12,8},{1,5},{5,1},{9,13},{13,9},{2,6},{6,2},{1... | collective-permute-start | bytes 589832 | tf_op jit(solution)/shard_map/proj3_core0/ppermute | solution.py:103
  28.4 3.3 %collective-permute-start.13 = (bf16[3,128,256]{2,1,0:T(8,128)(2,1)S(1)}, bf16[3,128,256]{2,1,0:T(8,128)(2,1)S(1)}, u32[]{:S(2)}, u32[]{:S(2)}) collective-permute-start(bf16[3,128,256]{2,1,0:T(8,128)(2,1)S(1)} %get-tuple-element.125), channel_id=1, source_target_pairs={{0,4},{4,0},{8,12},{12,8},{1,5},{5,1},{9,13},{13,9},{2,6},{6,2},{1... | collective-permute-start | bytes 589832 | tf_op jit(solution)/shard_map/proj3_core1/ppermute | solution.py:103
  28.9 7.4 %collective-permute-start.16 = (bf16[2,128,256]{2,1,0:T(8,128)(2,1)S(1)}, bf16[2,128,256]{2,1,0:T(8,128)(2,1)S(1)}, u32[]{:S(2)}, u32[]{:S(2)}) collective-permute-start(bf16[2,128,256]{2,1,0:T(8,128)(2,1)S(1)} %pad_maximum_fusion), channel_id=1, source_target_pairs={{0,8},{4,12},{8,0},{12,4},{1,9},{5,13},{9,1},{13,5},{2,10},{6,14},... | collective-permute-start | bytes 393224 | tf_op jit(solution)/shard_map/up_y/ppermute | solution.py:103
  29.6 10.6 %copy-start = (f32[3,3,1024]{2,1,0:T(4,128)S(1)}, f32[3,3,1024]{2,1,0:T(4,128)}, u32[]{:S(2)}) copy-start(f32[3,3,1024]{2,1,0:T(4,128)} %refs_3_.3) | copy-start | bytes 110596
  29.6 10.6 %copy-start.1 = (f32[7,1024]{1,0:T(8,128)S(1)}, f32[7,1024]{1,0:T(8,128)}, u32[]{:S(2)}) copy-start(f32[7,1024]{1,0:T(8,128)} %refs_4_.3) | copy-start | bytes 86020
  30.3 9.9 %collective-permute-start.18 = (bf16[1024,128]{1,0:T(8,128)(2,1)S(1)}, bf16[1024,128]{1,0:T(8,128)(2,1)S(1)}, u32[]{:S(2)}, u32[]{:S(2)}) collective-permute-start(bf16[1024,128]{1,0:T(8,128)(2,1)S(1)} %get-tuple-element.137.refs_2_), channel_id=1, source_target_pairs={{0,16},{16,0},{1,17},{17,1},{2,18},{18,2},{3,19},{19,3},{4,20},{20... | collective-permute-start | bytes 786440 | tf_op jit(solution)/shard_map/proj2_xt_x/ppermute | solution.py:103
  31.7 8.1 %collective-permute-start.14 = (bf16[3,128,256]{2,1,0:T(8,128)(2,1)S(1)}, bf16[3,128,256]{2,1,0:T(8,128)(2,1)S(1)}, u32[]{:S(2)}, u32[]{:S(2)}) collective-permute-start(bf16[3,128,256]{2,1,0:T(8,128)(2,1)S(1)} %get-tuple-element.127), channel_id=1, source_target_pairs={{0,8},{4,12},{8,0},{12,4},{1,9},{5,13},{9,1},{13,5},{2,10},{6,14},... | collective-permute-start | bytes 589832 | tf_op jit(solution)/shard_map/proj3_y/ppermute | solution.py:103
  36.4 8.8 %collective-permute-start.23 = (bf16[1024,128]{1,0:T(8,128)(2,1)S(1)}, bf16[1024,128]{1,0:T(8,128)(2,1)S(1)}, u32[]{:S(2)}, u32[]{:S(2)}) collective-permute-start(bf16[1024,128]{1,0:T(8,128)(2,1)S(1)} %get-tuple-element.144.refs_3_.refs_2_), channel_id=1, source_target_pairs={{0,16},{16,0},{1,17},{17,1},{2,18},{18,2},{3,19},{19,3},{4,20},{20... | collective-permute-start | bytes 786440 | tf_op jit(solution)/shard_map/proj3_xt_x/ppermute | solution.py:103
  40.8 6.3 %collective-permute-start.21 = (bf16[3,128,256]{2,1,0:T(8,128)(2,1)S(1)}, bf16[3,128,256]{2,1,0:T(8,128)(2,1)S(1)}, u32[]{:S(2)}, u32[]{:S(2)}) collective-permute-start(bf16[3,128,256]{2,1,0:T(8,128)(2,1)S(1)} %get-tuple-element.138.refs_5_), channel_id=1, source_target_pairs={{0,8},{4,12},{8,0},{12,4},{1,9},{5,13},{9,1},{13,5},{2,10},{6,14},... | collective-permute-start | bytes 589832 | tf_op jit(solution)/shard_map/g1_y/ppermute | solution.py:103
  43.2 10.1 %collective-permute-start.19 = (bf16[2,3,128,256]{3,2,1,0:T(8,128)(2,1)S(1)}, bf16[2,3,128,256]{3,2,1,0:T(8,128)(2,1)S(1)}, u32[]{:S(2)}, u32[]{:S(2)}) collective-permute-start(bf16[2,3,128,256]{3,2,1,0:T(8,128)(2,1)S(1)} %get-tuple-element.141.refs_0_), channel_id=1, source_target_pairs={{0,4},{4,0},{8,12},{12,8},{1,5},{5,1},{9,13},{13,9},{2,6},{6,2},{1... | collective-permute-start | bytes 1179656 | tf_op jit(solution)/shard_map/g30_core/ppermute | solution.py:103
  43.3 3.9 %collective-permute-start.28 = (bf16[3,128,256]{2,1,0:T(8,128)(2,1)S(1)}, bf16[3,128,256]{2,1,0:T(8,128)(2,1)S(1)}, u32[]{:S(2)}, u32[]{:S(2)}) collective-permute-start(bf16[3,128,256]{2,1,0:T(8,128)(2,1)S(1)} %get-tuple-element.142.refs_0_), channel_id=1, source_target_pairs={{0,4},{4,0},{8,12},{12,8},{1,5},{5,1},{9,13},{13,9},{2,6},{6,2},{1... | collective-permute-start | bytes 589832 | tf_op jit(solution)/shard_map/g2_core/ppermute | solution.py:103
  43.8 19.5 %collective-permute-start.25 = (bf16[4,3,128,256]{3,2,1,0:T(8,128)(2,1)S(1)}, bf16[4,3,128,256]{3,2,1,0:T(8,128)(2,1)S(1)}, u32[]{:S(2)}, u32[]{:S(2)}) collective-permute-start(bf16[4,3,128,256]{3,2,1,0:T(8,128)(2,1)S(1)} %get-tuple-element.140.refs_1_.refs_4_), channel_id=1, source_target_pairs={{0,16},{16,0},{1,17},{17,1},{2,18},{18,2},{3,19},{19,3},{4,20},{20... | collective-permute-start | bytes 2359304 | tf_op jit(solution)/shard_map/g_x/ppermute | solution.py:103
  45.3 2.6 %collective-permute-start.20 = (bf16[3,128,256]{2,1,0:T(8,128)(2,1)S(1)}, bf16[3,128,256]{2,1,0:T(8,128)(2,1)S(1)}, u32[]{:S(2)}, u32[]{:S(2)}) collective-permute-start(bf16[3,128,256]{2,1,0:T(8,128)(2,1)S(1)} %get-tuple-element.138.refs_5_), channel_id=1, source_target_pairs={{0,4},{4,0},{8,12},{12,8},{1,5},{5,1},{9,13},{13,9},{2,6},{6,2},{1... | collective-permute-start | bytes 589832 | tf_op jit(solution)/shard_map/g1_core/ppermute | solution.py:103
  47.2 1.4 %collective-permute-start.22 = (bf16[3,128,256]{2,1,0:T(8,128)(2,1)S(1)}, bf16[3,128,256]{2,1,0:T(8,128)(2,1)S(1)}, u32[]{:S(2)}, u32[]{:S(2)}) collective-permute-start(bf16[3,128,256]{2,1,0:T(8,128)(2,1)S(1)} %collective-permute-done.21.refs_2_.refs_3_), channel_id=1, source_target_pairs={{0,4},{4,0},{8,12},{12,8},{1,5},{5,1},{9,13},{13,9},{2,6},{6,2},{1... | collective-permute-start | bytes 589832 | tf_op jit(solution)/shard_map/gy1_core/ppermute | solution.py:103
  47.2 7.3 %collective-permute-start.26 = (bf16[3,128,256]{2,1,0:T(8,128)(2,1)S(1)}, bf16[3,128,256]{2,1,0:T(8,128)(2,1)S(1)}, u32[]{:S(2)}, u32[]{:S(2)}) collective-permute-start(bf16[3,128,256]{2,1,0:T(8,128)(2,1)S(1)} %get-tuple-element.148), channel_id=1, source_target_pairs={{0,8},{4,12},{8,0},{12,4},{1,9},{5,13},{9,1},{13,5},{2,10},{6,14},... | collective-permute-start | bytes 589832 | tf_op jit(solution)/shard_map/g2_y/ppermute | solution.py:103
  50.8 8.6 %collective-permute-start.29 = (bf16[128,1024]{1,0:T(8,128)(2,1)S(1)}, bf16[128,1024]{1,0:T(8,128)(2,1)S(1)}, u32[]{:S(2)}, u32[]{:S(2)}) collective-permute-start(bf16[128,1024]{1,0:T(8,128)(2,1)S(1)} %get-tuple-element.152), channel_id=1, source_target_pairs={{0,2},{2,3},{3,1},{1,0},{4,6},{6,7},{7,5},{5,4},{8,10},{10,11},{11... | collective-permute-start | bytes 786440 | tf_op jit(solution)/shard_map/share1/ppermute | solution.py:112
  53.2 10.9 %collective-permute-start.24 = (bf16[2,3,128,256]{3,2,1,0:T(8,128)(2,1)S(1)}, bf16[2,3,128,256]{3,2,1,0:T(8,128)(2,1)S(1)}, u32[]{:S(2)}, u32[]{:S(2)}) collective-permute-start(bf16[2,3,128,256]{3,2,1,0:T(8,128)(2,1)S(1)} %get-tuple-element.147), channel_id=1, source_target_pairs={{0,8},{4,12},{8,0},{12,4},{1,9},{5,13},{9,1},{13,5},{2,10},{6,14},... | collective-permute-start | bytes 1179656 | tf_op jit(solution)/shard_map/g30_y/ppermute | solution.py:103
  54.5 2.0 %collective-permute-start.27 = (bf16[3,128,256]{2,1,0:T(8,128)(2,1)S(1)}, bf16[3,128,256]{2,1,0:T(8,128)(2,1)S(1)}, u32[]{:S(2)}, u32[]{:S(2)}) collective-permute-start(bf16[3,128,256]{2,1,0:T(8,128)(2,1)S(1)} %collective-permute-done.26.refs_3_.refs_4_), channel_id=1, source_target_pairs={{0,4},{4,0},{8,12},{12,8},{1,5},{5,1},{9,13},{13,9},{2,6},{6,2},{1... | collective-permute-start | bytes 589832 | tf_op jit(solution)/shard_map/gy2_core/ppermute | solution.py:103
  63.3 7.6 %collective-permute-start.32 = (bf16[4,3,128,256]{3,2,1,0:T(8,128)(2,1)S(1)}, bf16[4,3,128,256]{3,2,1,0:T(8,128)(2,1)S(1)}, u32[]{:S(2)}, u32[]{:S(2)}) collective-permute-start(bf16[4,3,128,256]{3,2,1,0:T(8,128)(2,1)S(1)} %get-tuple-element.156.refs_0_.refs_4_), channel_id=1, source_target_pairs={{0,4},{4,0},{8,12},{12,8},{1,5},{5,1},{9,13},{13,9},{2,6},{6,2},{1... | collective-permute-start | bytes 2359304 | tf_op jit(solution)/shard_map/gx_core/ppermute | solution.py:103
  64.1 4.7 %collective-permute-start.30 = (bf16[2,3,128,256]{3,2,1,0:T(8,128)(2,1)S(1)}, bf16[2,3,128,256]{3,2,1,0:T(8,128)(2,1)S(1)}, u32[]{:S(2)}, u32[]{:S(2)}) collective-permute-start(bf16[2,3,128,256]{3,2,1,0:T(8,128)(2,1)S(1)} %get-tuple-element.159.refs_3_.refs_6_), channel_id=1, source_target_pairs={{0,4},{4,0},{8,12},{12,8},{1,5},{5,1},{9,13},{13,9},{2,6},{6,2},{1... | collective-permute-start | bytes 1179656 | tf_op jit(solution)/shard_map/gy30_core/ppermute | solution.py:103
  64.1 11.5 %collective-permute-start.33 = (bf16[2,3,128,256]{3,2,1,0:T(8,128)(2,1)S(1)}, bf16[2,3,128,256]{3,2,1,0:T(8,128)(2,1)S(1)}, u32[]{:S(2)}, u32[]{:S(2)}) collective-permute-start(bf16[2,3,128,256]{3,2,1,0:T(8,128)(2,1)S(1)} %get-tuple-element.167), channel_id=1, source_target_pairs={{0,8},{4,12},{8,0},{12,4},{1,9},{5,13},{9,1},{13,5},{2,10},{6,14},... | collective-permute-start | bytes 1179656 | tf_op jit(solution)/shard_map/gx12_y/ppermute | solution.py:103
  65.3 11.2 %collective-permute-start.35 = (bf16[2,3,128,256]{3,2,1,0:T(8,128)(2,1)S(1)}, bf16[2,3,128,256]{3,2,1,0:T(8,128)(2,1)S(1)}, u32[]{:S(2)}, u32[]{:S(2)}) collective-permute-start(bf16[2,3,128,256]{3,2,1,0:T(8,128)(2,1)S(1)} %get-tuple-element.159.refs_3_.refs_6_), channel_id=1, source_target_pairs={{0,16},{16,0},{1,17},{17,1},{2,18},{18,2},{3,19},{19,3},{4,20},{20... | collective-permute-start | bytes 1179656 | tf_op jit(solution)/shard_map/gy30_x/ppermute | solution.py:103
  66.8 8.6 %collective-permute-start.31 = (bf16[128,1024]{1,0:T(8,128)(2,1)S(1)}, bf16[128,1024]{1,0:T(8,128)(2,1)S(1)}, u32[]{:S(2)}, u32[]{:S(2)}) collective-permute-start(bf16[128,1024]{1,0:T(8,128)(2,1)S(1)} %get-tuple-element.163), channel_id=1, source_target_pairs={{0,2},{2,3},{3,1},{1,0},{4,6},{6,7},{7,5},{5,4},{8,10},{10,11},{11... | collective-permute-start | bytes 786440 | tf_op jit(solution)/shard_map/share2/ppermute | solution.py:112
  76.5 2.4 %collective-permute-start.36 = (bf16[2,3,128,256]{3,2,1,0:T(8,128)(2,1)S(1)}, bf16[2,3,128,256]{3,2,1,0:T(8,128)(2,1)S(1)}, u32[]{:S(2)}, u32[]{:S(2)}) collective-permute-start(bf16[2,3,128,256]{3,2,1,0:T(8,128)(2,1)S(1)} %get-tuple-element.170.refs_7_), channel_id=1, source_target_pairs={{0,4},{4,0},{8,12},{12,8},{1,5},{5,1},{9,13},{13,9},{2,6},{6,2},{1... | collective-permute-start | bytes 1179656 | tf_op jit(solution)/shard_map/gxy30_core/ppermute | solution.py:103
  76.5 2.4 %collective-permute-start.37 = (bf16[2,3,128,256]{3,2,1,0:T(8,128)(2,1)S(1)}, bf16[2,3,128,256]{3,2,1,0:T(8,128)(2,1)S(1)}, u32[]{:S(2)}, u32[]{:S(2)}) collective-permute-start(bf16[2,3,128,256]{3,2,1,0:T(8,128)(2,1)S(1)} %get-tuple-element.171.refs_8_), channel_id=1, source_target_pairs={{0,4},{4,0},{8,12},{12,8},{1,5},{5,1},{9,13},{13,9},{2,6},{6,2},{1... | collective-permute-start | bytes 1179656 | tf_op jit(solution)/shard_map/gxy12_core/ppermute | solution.py:103
  77.0 8.2 %collective-permute-start.34 = (bf16[128,1024]{1,0:T(8,128)(2,1)S(1)}, bf16[128,1024]{1,0:T(8,128)(2,1)S(1)}, u32[]{:S(2)}, u32[]{:S(2)}) collective-permute-start(bf16[128,1024]{1,0:T(8,128)(2,1)S(1)} %get-tuple-element.168), channel_id=1, source_target_pairs={{0,2},{2,3},{3,1},{1,0},{4,6},{6,7},{7,5},{5,4},{8,10},{10,11},{11... | collective-permute-start | bytes 786440 | tf_op jit(solution)/shard_map/share3/ppermute | solution.py:112
